TPU v7x, 32 devices: a whole 2x2x4 slice. The times are simulated.
32 devices in a mesh: seq: 16 (over z, y, core), chan: 2 (over x).
Axes of the slice: x: 2, y: 2, z: 4, core: 2. Of those that a mesh axis runs over, the one named last changes fastest.
Arguments:
- inputs: bfloat16 [2048, 8192], P('seq', 'chan'), may hold values from -256 to 256
- gating: bfloat16 [2048, 8192], P('seq', 'chan'), may hold values from -6 to 6
- long_filter: bfloat16 [513, 8192], P(None, 'chan'), may hold values from -0.25 to 0.25
- skip_scale: float32 [8192], P('chan'), may hold values from 0.5 to 1.5
Outputs:
- gated: bfloat16 [2048, 8192], P('seq', 'chan')
All inputs are finite; a program needn't handle non-finite values.
Results may differ from a plain program's by a relative error of at most 0.0049.
Values may be sent and summed in bfloat16 or wider, within the bound.
No kernel may reach another device: no remote copies, remote signals or barrier semaphores. Data moves between devices by JAX's collectives and lax.ppermute only.
A program may use at most 128 MiB of HBM per device.

v0:
```python
import functools

import jax
import jax.numpy as jnp
import ml_dtypes
import numpy as np
from jax import lax
from jax.experimental import pallas as pl
from jax.experimental.pallas import tpu as pltpu
from jax.sharding import PartitionSpec as P

BF16 = jnp.bfloat16
F32 = jnp.float32
EPS = 1e-06
GROUP = 4
VMEM_LIMIT = 48 * 2**20


def split(table):
    high = table.astype(ml_dtypes.bfloat16)
    low = (table - high.astype(np.float64)).astype(ml_dtypes.bfloat16)
    return high, low


def tables(rows):
    index = np.concatenate([np.arange(0, rows, 2), np.arange(1, rows, 2)])
    turns = (index + 0.5)[:, None] * np.arange(rows)[None, :] / (2 * rows)
    angle = 2 * np.pi * turns
    forward = np.concatenate([np.cos(angle), -np.sin(angle)], 0)
    back = np.concatenate([np.cos(angle), -np.sin(angle)], 0).T / rows
    f_high, f_low = split(forward)
    b_high, b_low = split(back)
    return np.concatenate([f_high, f_low], 1), np.concatenate([b_high, b_low, b_high], 1)


def dot(left, right):
    return jnp.dot(left, right, preferred_element_type=F32)


def spectrum(table, block):
    both = dot(table, jnp.concatenate([block, block], 0))
    half = both.shape[0] // 2
    return both[:half], both[half:]


def delayed(real, imag):
    half = real.shape[0] // 2
    return (
        jnp.concatenate([-imag[:half], imag[half:]], 0),
        jnp.concatenate([real[:half], -real[half:]], 0),
    )


def plus(left, right):
    return left[0] + right[0], left[1] + right[1]


def times(left, right):
    return left[0] * right[0] - left[1] * right[1], left[0] * right[1] + left[1] * right[0]


def pick(flag, left, right):
    return jnp.where(flag, left[0], right[0]), jnp.where(flag, left[1], right[1])


def early_body(core, forward, own, far, side, taps, acc, mid, other):
    rows = own.shape[0]
    table = forward[...]
    first = core[0] == 0
    g = [spectrum(table, taps[j * rows : (j + 1) * rows, :]) for j in range(GROUP)]
    h = [g[0]] + [plus(g[j], delayed(*g[j - 1])) for j in range(1, GROUP)] + [delayed(*g[GROUP - 1])]
    total = times(spectrum(table, own[...]), h[0])
    total = plus(total, times(spectrum(table, far[...]), h[4]))
    total = plus(total, times(spectrum(table, side[...]), pick(first, h[3], h[1])))
    last = pick(first, h[1], h[3])
    for ref, value in ((acc, total), (mid, h[2]), (other, last)):
        ref[:rows, :] = value[0]
        ref[rows:, :] = value[1]


def late_body(forward, back, near, swapped, own, far, gate, scales, acc, mid, other, *rest):
    out = rest[-1]
    rows = own.shape[0]
    table = forward[...]
    total = (acc[:rows, :], acc[rows:, :])
    total = plus(total, times(spectrum(table, near[...]), (mid[:rows, :], mid[rows:, :])))
    total = plus(total, times(spectrum(table, swapped[...]), (other[:rows, :], other[rows:, :])))
    total = jnp.concatenate(total, 0)
    high = total.astype(BF16)
    low = (total - high.astype(F32)).astype(BF16)
    conv = dot(back[...], jnp.concatenate([high, high, low], 0))
    conv = conv + scales[0:1, :] * far[...].astype(F32)
    mixed = conv + scales[1:2, :] * own[...].astype(F32)
    out[...] = (gate[...].astype(F32) * mixed).astype(BF16)


def whole(array):
    return pl.BlockSpec(array.shape, lambda i: (0,) * array.ndim)


def columns(rows, tile, start=0):
    return pl.BlockSpec((rows, tile), lambda i: (0, start // tile + i))


PARAMS = pltpu.CompilerParams(vmem_limit_bytes=VMEM_LIMIT)


def early(core, forward, own, far, side, long_filter, start, tile):
    rows, width = own.shape
    spec = columns(2 * rows, tile)
    shape = jax.ShapeDtypeStruct((2 * rows, width), F32)
    return pl.pallas_call(
        early_body,
        grid=(width // tile,),
        in_specs=[pl.BlockSpec(memory_space=pltpu.SMEM), whole(forward)]
        + [columns(rows, tile)] * 3
        + [columns(GROUP * rows, tile, start)],
        out_specs=[spec] * 3,
        out_shape=[shape] * 3,
        compiler_params=PARAMS,
    )(core, forward, own, far, side, long_filter)


def late(forward, back, near, swapped, own, far, gate, scales, kept, start, tile, out):
    rows, width = own.shape
    spec = columns(2 * rows, tile)
    operands = [forward, back, near, swapped, own, far, gate, scales, *kept]
    in_specs = (
        [whole(forward), whole(back)]
        + [columns(rows, tile)] * 4
        + [columns(rows, tile, start), columns(2, tile, start)]
        + [spec] * 3
    )
    aliases = {}
    if out is not None:
        aliases = {len(operands): 0}
        operands.append(out)
        in_specs.append(pl.BlockSpec(memory_space=pl.ANY))
    return pl.pallas_call(
        late_body,
        grid=(width // tile,),
        in_specs=in_specs,
        out_specs=columns(rows, tile, start),
        out_shape=jax.ShapeDtypeStruct(gate.shape, BF16),
        input_output_aliases=aliases,
        compiler_params=PARAMS,
    )(*operands)


def shifted(value, steps):
    count = lax.axis_size("seq")
    return lax.ppermute(value, "seq", [(s, s + steps) for s in range(count - steps)])


def swapped_with(value, axis, bit):
    return lax.ppermute(value, axis, [(s, s ^ bit) for s in range(lax.axis_size(axis))])


def sum_over(value, axis):
    count = lax.axis_size(axis)
    if count & (count - 1):
        return lax.psum(value, axis)
    bit = 1
    while bit < count:
        value = value + swapped_with(value, axis, bit)
        bit *= 2
    return value


def on_device(inputs, gating, long_filter, skip_scale):
    rows, channels = inputs.shape
    place = lax.axis_index("seq")
    core = place % 2
    on_low = place // 2 % 2 == 0
    forward, back = (jnp.asarray(table) for table in tables(rows))

    values = inputs.astype(F32)
    squares = sum_over(jnp.sum(values * values, axis=1, keepdims=True), "chan")
    total_channels = channels * lax.axis_size("chan")
    normed = (values * lax.rsqrt(squares / total_channels + EPS)).astype(BF16)
    scales = jnp.stack([long_filter[-1].astype(F32), skip_scale])

    tile = channels // 8
    widths = [2 * tile, 3 * tile, 3 * tile]
    starts = [0, 2 * tile, 5 * tile]
    own = [normed[:, s : s + w] for s, w in zip(starts, widths)]
    far = [shifted(block, 4) for block in own]
    near = [swapped_with(jnp.where(on_low, own[k], far[k]), "seq", 2) for k in range(2)]
    near.append(shifted(own[2], 2))
    out = None
    core_arg = core.astype(jnp.int32).reshape(1)
    for k in range(3):
        side = swapped_with(jnp.where(core == 0, own[k], far[k]), "seq", 1)
        kept = early(core_arg, forward, own[k], far[k], side, long_filter, starts[k], tile)
        other = swapped_with(near[k], "seq", 1)
        out = late(forward, back, near[k], other, own[k], far[k], gating, scales, kept, starts[k], tile, out)
    return out


def solution(mesh):
    in_specs = (P("seq", "chan"), P("seq", "chan"), P(None, "chan"), P("chan"))
    out_specs = P("seq", "chan")
    return jax.shard_map(
        on_device, mesh=mesh, in_specs=in_specs, out_specs=out_specs, check_vma=False
    )
```

profile of v0, /device:TPU:17, one launch (start us, length us, event | category | flops | bytes accessed | tf_op | source)
XLA Modules:
  0.0 75.0 jit_solution(5657614996916801733)
XLA Ops:
  0.0 1.5 %fusion = f32[128]{0:T(128)S(1)} fusion(bf16[128,4096]{1,0:T(8,128)(2,1)} %param.6), kind=kLoop, calls=%fused_computation.2 | loop fusion | flops 1572736 | bytes 1049088 | tf_op jit(solution)/shard_map/reduce_sum | solution.py:178
  1.5 1.3 %collective-permute-start = (f32[128,1]{0,1:T(1,128)S(1)}, f32[128,1]{0,1:T(1,128)S(1)}, u32[]{:S(2)}, u32[]{:S(2)}) collective-permute-start(f32[128,1]{0,1:T(1,128)S(1)} %bitcast.7), channel_id=1, source_target_pairs={{0,1},{1,0},{2,3},{3,2},{4,5},{5,4},{6,7},{7,6},{8,9},{9,8},{10,11... | collective-permute-start | bytes 1544 | tf_op jit(solution)/shard_map/ppermute | solution.py:156
  2.8 1.2 %collective-permute-done = f32[128,1]{0,1:T(1,128)S(1)} collective-permute-done((f32[128,1]{0,1:T(1,128)S(1)}, f32[128,1]{0,1:T(1,128)S(1)}, u32[]{:S(2)}, u32[]{:S(2)}) %collective-permute-start) | collective-permute-done | bytes 544 | tf_op jit(solution)/shard_map/ppermute | solution.py:156
  4.0 1.5 %fusion.1 = bf16[128,4096]{1,0:T(8,128)(2,1)S(1)} fusion(bf16[128,4096]{1,0:T(8,128)(2,1)} %param.6, f32[128]{0:T(128)S(1)} %rsqrt_bitcast_fusion), kind=kLoop, calls=%fused_computation.3 | loop fusion | flops 1572864 | bytes 2097664 | tf_op jit(solution)/shard_map/convert_element_type | solution.py:180
  5.5 3.2 %collective-permute-start.9 = (bf16[128,1024]{1,0:T(8,128)(2,1)S(1)}, bf16[128,1024]{1,0:T(8,128)(2,1)S(1)}, u32[]{:S(2)}, u32[]{:S(2)}) collective-permute-start(bf16[128,1024]{1,0:T(8,128)(2,1)S(1)} %slice.18.own), channel_id=1, source_target_pairs={{0,8},{2,10},{4,12},{6,14},{8,16},{10,18},{12,20},{14,22},{16,24},... | collective-permute-start | bytes 786440 | tf_op jit(solution)/shard_map/ppermute | solution.py:152
  8.7 1.9 %collective-permute-start.5 = (bf16[128,1536]{1,0:T(8,128)(2,1)S(1)}, bf16[128,1536]{1,0:T(8,128)(2,1)S(1)}, u32[]{:S(2)}, u32[]{:S(2)}) collective-permute-start(bf16[128,1536]{1,0:T(8,128)(2,1)S(1)} %slice.17.own), channel_id=1, source_target_pairs={{0,8},{2,10},{4,12},{6,14},{8,16},{10,18},{12,20},{14,22},{16,24},... | collective-permute-start | bytes 1179656 | tf_op jit(solution)/shard_map/ppermute | solution.py:152
  10.7 0.0 copy-start.5
  10.7 0.0 copy-start.1
  10.7 2.6 %collective-permute-done.9.far = bf16[128,1024]{1,0:T(8,128)(2,1)S(1)} collective-permute-done((bf16[128,1024]{1,0:T(8,128)(2,1)S(1)}, bf16[128,1024]{1,0:T(8,128)(2,1)S(1)}, u32[]{:S(2)}, u32[]{:S(2)}) %collective-permute-start.9) | collective-permute-done | bytes 262176 | tf_op jit(solution)/shard_map/ppermute | solution.py:152
  13.4 1.3 %collective-permute-start.10 = (bf16[128,1024]{1,0:T(8,128)(2,1)S(1)}, bf16[128,1024]{1,0:T(8,128)(2,1)S(1)}, u32[]{:S(2)}, u32[]{:S(2)}) collective-permute-start(bf16[128,1024]{1,0:T(8,128)(2,1)S(1)} %get-tuple-element.26), channel_id=1, source_target_pairs={{0,4},{2,6},{4,0},{6,2},{8,12},{10,14},{12,8},{14,10},{16,20},{18,... | collective-permute-start | bytes 786440 | tf_op jit(solution)/shard_map/ppermute | solution.py:156
  14.7 7.1 %collective-permute-done.5.far = bf16[128,1536]{1,0:T(8,128)(2,1)S(1)} collective-permute-done((bf16[128,1536]{1,0:T(8,128)(2,1)S(1)}, bf16[128,1536]{1,0:T(8,128)(2,1)S(1)}, u32[]{:S(2)}, u32[]{:S(2)}) %collective-permute-start.5) | collective-permute-done | bytes 393248 | tf_op jit(solution)/shard_map/ppermute | solution.py:152
  21.8 0.1 broadcast_select_fusion.1
  21.9 3.2 %collective-permute-start.3 = (bf16[128,1536]{1,0:T(8,128)(2,1)S(1)}, bf16[128,1536]{1,0:T(8,128)(2,1)S(1)}, u32[]{:S(2)}, u32[]{:S(2)}) collective-permute-start(bf16[128,1536]{1,0:T(8,128)(2,1)S(1)} %get-tuple-element.27.own), channel_id=1, source_target_pairs={{0,8},{2,10},{4,12},{6,14},{8,16},{10,18},{12,20},{14,22},{16,24},... | collective-permute-start | bytes 1179656 | tf_op jit(solution)/shard_map/ppermute | solution.py:152
  25.1 0.9 %slice_convert_fusion = f32[1,4096]{1,0:T(1,128)S(1)} fusion(bf16[513,4096]{1,0:T(8,128)(2,1)} %taps.5), kind=kLoop, calls=%fused_computation.10 | loop fusion | flops 4096 | bytes 24576 | tf_op jit(solution)/shard_map/convert_element_type | solution.py:181
  25.9 3.1 %collective-permute-start.12 = (bf16[128,1024]{1,0:T(8,128)(2,1)S(1)}, bf16[128,1024]{1,0:T(8,128)(2,1)S(1)}, u32[]{:S(2)}, u32[]{:S(2)}) collective-permute-start(bf16[128,1024]{1,0:T(8,128)(2,1)S(1)} %get-tuple-element.25), channel_id=1, source_target_pairs={{0,2},{2,0},{4,6},{6,4},{8,10},{10,8},{12,14},{14,12},{16,18},{18,... | collective-permute-start | bytes 786440 | tf_op jit(solution)/shard_map/ppermute | solution.py:156
  29.0 3.1 %collective-permute-start.1 = (bf16[128,1536]{1,0:T(8,128)(2,1)S(1)}, bf16[128,1536]{1,0:T(8,128)(2,1)S(1)}, u32[]{:S(2)}, u32[]{:S(2)}) collective-permute-start(bf16[128,1536]{1,0:T(8,128)(2,1)S(1)} %get-tuple-element.27.own), channel_id=1, source_target_pairs={{0,4},{2,6},{4,8},{6,10},{8,12},{10,14},{12,16},{14,18},{16,20},{1... | collective-permute-start | bytes 1179656 | tf_op jit(solution)/shard_map/ppermute | solution.py:152
  32.2 0.4 collective-permute-start.8
  32.5 0.0 collective-permute-done.10.near
  32.5 0.0 collective-permute-start.6
  32.6 2.7 %collective-permute-start.11 = (bf16[128,1024]{1,0:T(8,128)(2,1)S(1)}, bf16[128,1024]{1,0:T(8,128)(2,1)S(1)}, u32[]{:S(2)}, u32[]{:S(2)}) collective-permute-start(bf16[128,1024]{1,0:T(8,128)(2,1)S(1)} %collective-permute-done.10.near), channel_id=1, source_target_pairs={{0,2},{2,0},{4,6},{6,4},{8,10},{10,8},{12,14},{14,12},{16,18},{18,... | collective-permute-start | bytes 786440 | tf_op jit(solution)/shard_map/ppermute | solution.py:156
  35.3 0.1 collective-permute-start.4
  35.4 16.0 %collective-permute-done.6.near = bf16[128,1536]{1,0:T(8,128)(2,1)S(1)} collective-permute-done((bf16[128,1536]{1,0:T(8,128)(2,1)S(1)}, bf16[128,1536]{1,0:T(8,128)(2,1)S(1)}, u32[]{:S(2)}, u32[]{:S(2)}) %collective-permute-start.6) | collective-permute-done | bytes 393248 | tf_op jit(solution)/shard_map/ppermute | solution.py:156
  51.4 0.7 collective-permute-start.7
  52.2 0.0 collective-permute-start.2
  52.2 2.9 %shard_map.66 = (f32[256,1024]{1,0:T(8,128)S(1)}, f32[256,1024]{1,0:T(8,128)S(1)}, f32[256,1024]{1,0:T(8,128)S(1)}) custom-call(s32[1]{0:T(128)} %bitcast.3.core, bf16[256,256]{1,0:T(8,128)(2,1)S(1)} %copy-done.1, bf16[128,1024]{1,0:T(8,128)(2,1)S(1)} %slice.18.own, bf16[128,1024]{1,0:T(8,128)(2,1)S(1)} %collective-permute-done.9.far, ...), custom_call_target="tpu_custom_call" | custom-call | tf_op jit(solution)/shard_map/pallas_call | solution.py:112
  55.1 0.0 copy-start
  55.2 0.0 copy-start.2
  55.2 4.1 %shard_map.65 = (f32[256,1536]{1,0:T(8,128)S(1)}, f32[256,1536]{1,0:T(8,128)S(1)}, f32[256,1536]{1,0:T(8,128)S(1)}) custom-call(s32[1]{0:T(128)} %bitcast.3.core, bf16[256,256]{1,0:T(8,128)(2,1)S(1)} %copy-done.1, bf16[128,1536]{1,0:T(8,128)(2,1)S(1)} %slice.17.own, bf16[128,1536]{1,0:T(8,128)(2,1)S(1)} %collective-permute-done.5.far, ...), custom_call_target="tpu_custom_call" | custom-call | tf_op jit(solution)/shard_map/pallas_call | solution.py:112
  59.3 2.4 %shard_map.67.rest_0_ = bf16[128,4096]{1,0:T(8,128)(2,1)} custom-call(bf16[256,256]{1,0:T(8,128)(2,1)S(1)} %copy-done.1, bf16[128,768]{1,0:T(8,128)(2,1)S(1)} %copy-done.2, bf16[128,1024]{1,0:T(8,128)(2,1)S(1)} %collective-permute-done.10.near, bf16[128,1024]{1,0:T(8,128)(2,1)S(1)} %collective-permute-done.11.swapped, bf16[128,1024]{1,0:T(8,128)(2,1)S(1)} %slice.18.own, ...), custom_call_target="tpu_custom_call" | custom-call | tf_op jit(solution)/shard_map/pallas_call | solution.py:139
  61.7 4.0 %shard_map.64 = (f32[256,1536]{1,0:T(8,128)S(1)}, f32[256,1536]{1,0:T(8,128)S(1)}, f32[256,1536]{1,0:T(8,128)S(1)}) custom-call(s32[1]{0:T(128)} %bitcast.3.core, bf16[256,256]{1,0:T(8,128)(2,1)S(1)} %copy-done.1, bf16[128,1536]{1,0:T(8,128)(2,1)S(1)} %get-tuple-element.27.own, bf16[128,1536]{1,0:T(8,128)(2,1)S(1)} %collective-permute-done.3.far, ...), custom_call_target="tpu_custom_call" | custom-call | tf_op jit(solution)/shard_map/pallas_call | solution.py:112
  65.7 4.8 %shard_map.68.rest_0_ = bf16[128,4096]{1,0:T(8,128)(2,1)} custom-call(bf16[256,256]{1,0:T(8,128)(2,1)S(1)} %copy-done.1, bf16[128,768]{1,0:T(8,128)(2,1)S(1)} %copy-done.2, bf16[128,1536]{1,0:T(8,128)(2,1)S(1)} %collective-permute-done.6.near, bf16[128,1536]{1,0:T(8,128)(2,1)S(1)} %collective-permute-done.7.swapped, ...), custom_call_target="tpu_custom_call", output_to_operand_aliasing={{}: (11, {})} | custom-call | tf_op jit(solution)/shard_map/pallas_call | solution.py:139
  70.5 4.4 %shard_map.69 = bf16[128,4096]{1,0:T(8,128)(2,1)} custom-call(bf16[256,256]{1,0:T(8,128)(2,1)S(1)} %copy-done.1, bf16[128,768]{1,0:T(8,128)(2,1)S(1)} %copy-done.2, bf16[128,1536]{1,0:T(8,128)(2,1)S(1)} %collective-permute-done.1.near, bf16[128,1536]{1,0:T(8,128)(2,1)S(1)} %collective-permute-done.2.swapped, ...), custom_call_target="tpu_custom_call", output_to_operand_aliasing={{}: (11, {})} | custom-call | tf_op jit(solution)/shard_map/pallas_call | solution.py:139
  (22 shorter events, 0.2 us)
Async XLA Ops:
  1.5 2.4 %collective-permute-start = (f32[128,1]{0,1:T(1,128)S(1)}, f32[128,1]{0,1:T(1,128)S(1)}, u32[]{:S(2)}, u32[]{:S(2)}) collective-permute-start(f32[128,1]{0,1:T(1,128)S(1)} %bitcast.7), channel_id=1, source_target_pairs={{0,1},{1,0},{2,3},{3,2},{4,5},{5,4},{6,7},{7,6},{8,9},{9,8},{10,11... | collective-permute-start | bytes 1544 | tf_op jit(solution)/shard_map/ppermute | solution.py:156
  5.5 7.9 %collective-permute-start.9 = (bf16[128,1024]{1,0:T(8,128)(2,1)S(1)}, bf16[128,1024]{1,0:T(8,128)(2,1)S(1)}, u32[]{:S(2)}, u32[]{:S(2)}) collective-permute-start(bf16[128,1024]{1,0:T(8,128)(2,1)S(1)} %slice.18.own), channel_id=1, source_target_pairs={{0,8},{2,10},{4,12},{6,14},{8,16},{10,18},{12,20},{14,22},{16,24},... | collective-permute-start | bytes 786440 | tf_op jit(solution)/shard_map/ppermute | solution.py:152
  8.7 13.0 %collective-permute-start.5 = (bf16[128,1536]{1,0:T(8,128)(2,1)S(1)}, bf16[128,1536]{1,0:T(8,128)(2,1)S(1)}, u32[]{:S(2)}, u32[]{:S(2)}) collective-permute-start(bf16[128,1536]{1,0:T(8,128)(2,1)S(1)} %slice.17.own), channel_id=1, source_target_pairs={{0,8},{2,10},{4,12},{6,14},{8,16},{10,18},{12,20},{14,22},{16,24},... | collective-permute-start | bytes 1179656 | tf_op jit(solution)/shard_map/ppermute | solution.py:152
  10.7 41.5 %copy-start.5 = (f32[4096]{0:T(1024)S(1)}, f32[4096]{0:T(1024)}, u32[]{:S(2)}) copy-start(f32[4096]{0:T(1024)} %param.9) | copy-start | bytes 49156
  10.7 41.5 %copy-start.1 = (bf16[256,256]{1,0:T(8,128)(2,1)S(1)}, bf16[256,256]{1,0:T(8,128)(2,1)}, u32[]{:S(2)}) copy-start(bf16[256,256]{1,0:T(8,128)(2,1)} %constant.46.clone.forward) | copy-start | bytes 393220
  13.4 19.1 %collective-permute-start.10 = (bf16[128,1024]{1,0:T(8,128)(2,1)S(1)}, bf16[128,1024]{1,0:T(8,128)(2,1)S(1)}, u32[]{:S(2)}, u32[]{:S(2)}) collective-permute-start(bf16[128,1024]{1,0:T(8,128)(2,1)S(1)} %get-tuple-element.26), channel_id=1, source_target_pairs={{0,4},{2,6},{4,0},{6,2},{8,12},{10,14},{12,8},{14,10},{16,20},{18,... | collective-permute-start | bytes 786440 | tf_op jit(solution)/shard_map/ppermute | solution.py:156
  21.9 10.7 %collective-permute-start.3 = (bf16[128,1536]{1,0:T(8,128)(2,1)S(1)}, bf16[128,1536]{1,0:T(8,128)(2,1)S(1)}, u32[]{:S(2)}, u32[]{:S(2)}) collective-permute-start(bf16[128,1536]{1,0:T(8,128)(2,1)S(1)} %get-tuple-element.27.own), channel_id=1, source_target_pairs={{0,8},{2,10},{4,12},{6,14},{8,16},{10,18},{12,20},{14,22},{16,24},... | collective-permute-start | bytes 1179656 | tf_op jit(solution)/shard_map/ppermute | solution.py:152
  25.9 9.4 %collective-permute-start.12 = (bf16[128,1024]{1,0:T(8,128)(2,1)S(1)}, bf16[128,1024]{1,0:T(8,128)(2,1)S(1)}, u32[]{:S(2)}, u32[]{:S(2)}) collective-permute-start(bf16[128,1024]{1,0:T(8,128)(2,1)S(1)} %get-tuple-element.25), channel_id=1, source_target_pairs={{0,2},{2,0},{4,6},{6,4},{8,10},{10,8},{12,14},{14,12},{16,18},{18,... | collective-permute-start | bytes 786440 | tf_op jit(solution)/shard_map/ppermute | solution.py:156
  29.0 23.1 %collective-permute-start.1 = (bf16[128,1536]{1,0:T(8,128)(2,1)S(1)}, bf16[128,1536]{1,0:T(8,128)(2,1)S(1)}, u32[]{:S(2)}, u32[]{:S(2)}) collective-permute-start(bf16[128,1536]{1,0:T(8,128)(2,1)S(1)} %get-tuple-element.27.own), channel_id=1, source_target_pairs={{0,4},{2,6},{4,8},{6,10},{8,12},{10,14},{12,16},{14,18},{16,20},{1... | collective-permute-start | bytes 1179656 | tf_op jit(solution)/shard_map/ppermute | solution.py:152
  32.2 23.0 %collective-permute-start.8 = (bf16[128,1536]{1,0:T(8,128)(2,1)S(1)}, bf16[128,1536]{1,0:T(8,128)(2,1)S(1)}, u32[]{:S(2)}, u32[]{:S(2)}) collective-permute-start(bf16[128,1536]{1,0:T(8,128)(2,1)S(1)} %get-tuple-element.23), channel_id=1, source_target_pairs={{0,2},{2,0},{4,6},{6,4},{8,10},{10,8},{12,14},{14,12},{16,18},{18,... | collective-permute-start | bytes 1179656 | tf_op jit(solution)/shard_map/ppermute | solution.py:156
  32.5 18.9 %collective-permute-start.6 = (bf16[128,1536]{1,0:T(8,128)(2,1)S(1)}, bf16[128,1536]{1,0:T(8,128)(2,1)S(1)}, u32[]{:S(2)}, u32[]{:S(2)}) collective-permute-start(bf16[128,1536]{1,0:T(8,128)(2,1)S(1)} %get-tuple-element.24), channel_id=1, source_target_pairs={{0,4},{2,6},{4,0},{6,2},{8,12},{10,14},{12,8},{14,10},{16,20},{18,... | collective-permute-start | bytes 1179656 | tf_op jit(solution)/shard_map/ppermute | solution.py:156
  32.6 26.7 %collective-permute-start.11 = (bf16[128,1024]{1,0:T(8,128)(2,1)S(1)}, bf16[128,1024]{1,0:T(8,128)(2,1)S(1)}, u32[]{:S(2)}, u32[]{:S(2)}) collective-permute-start(bf16[128,1024]{1,0:T(8,128)(2,1)S(1)} %collective-permute-done.10.near), channel_id=1, source_target_pairs={{0,2},{2,0},{4,6},{6,4},{8,10},{10,8},{12,14},{14,12},{16,18},{18,... | collective-permute-start | bytes 786440 | tf_op jit(solution)/shard_map/ppermute | solution.py:156
  35.3 26.4 %collective-permute-start.4 = (bf16[128,1536]{1,0:T(8,128)(2,1)S(1)}, bf16[128,1536]{1,0:T(8,128)(2,1)S(1)}, u32[]{:S(2)}, u32[]{:S(2)}) collective-permute-start(bf16[128,1536]{1,0:T(8,128)(2,1)S(1)} %broadcast_select_fusion.2), channel_id=1, source_target_pairs={{0,2},{2,0},{4,6},{6,4},{8,10},{10,8},{12,14},{14,12},{16,18},{18,... | collective-permute-start | bytes 1179656 | tf_op jit(solution)/shard_map/ppermute | solution.py:156
  51.4 14.3 %collective-permute-start.7 = (bf16[128,1536]{1,0:T(8,128)(2,1)S(1)}, bf16[128,1536]{1,0:T(8,128)(2,1)S(1)}, u32[]{:S(2)}, u32[]{:S(2)}) collective-permute-start(bf16[128,1536]{1,0:T(8,128)(2,1)S(1)} %collective-permute-done.6.near), channel_id=1, source_target_pairs={{0,2},{2,0},{4,6},{6,4},{8,10},{10,8},{12,14},{14,12},{16,18},{18,... | collective-permute-start | bytes 1179656 | tf_op jit(solution)/shard_map/ppermute | solution.py:156
  52.2 18.4 %collective-permute-start.2 = (bf16[128,1536]{1,0:T(8,128)(2,1)S(1)}, bf16[128,1536]{1,0:T(8,128)(2,1)S(1)}, u32[]{:S(2)}, u32[]{:S(2)}) collective-permute-start(bf16[128,1536]{1,0:T(8,128)(2,1)S(1)} %collective-permute-done.1.near), channel_id=1, source_target_pairs={{0,2},{2,0},{4,6},{6,4},{8,10},{10,8},{12,14},{14,12},{16,18},{18,... | collective-permute-start | bytes 1179656 | tf_op jit(solution)/shard_map/ppermute | solution.py:156
  55.1 4.1 %copy-start = (bf16[128,4096]{1,0:T(8,128)(2,1)S(1)}, bf16[128,4096]{1,0:T(8,128)(2,1)}, u32[]{:S(2)}) copy-start(bf16[128,4096]{1,0:T(8,128)(2,1)} %gate.5) | copy-start | bytes 3145732
  55.2 4.1 %copy-start.2 = (bf16[128,768]{1,0:T(8,128)(2,1)S(1)}, bf16[128,768]{1,0:T(8,128)(2,1)}, u32[]{:S(2)}) copy-start(bf16[128,768]{1,0:T(8,128)(2,1)} %constant.47.clone.back) | copy-start | bytes 589828
  59.3 2.5 %copy-start.3 = (f32[256,1536]{1,0:T(8,128)}, f32[256,1536]{1,0:T(8,128)S(1)}, u32[]{:S(2)}) copy-start(f32[256,1536]{1,0:T(8,128)S(1)} %get-tuple-element.19.other) | copy-start | bytes 4718596
  65.7 4.9 %copy-start.4 = (f32[256,1536]{1,0:T(8,128)}, f32[256,1536]{1,0:T(8,128)S(1)}, u32[]{:S(2)}) copy-start(f32[256,1536]{1,0:T(8,128)S(1)} %get-tuple-element.16.other) | copy-start | bytes 4718596
where the time goes:
time: 75.5 us; the launch traced here: 75 us
  waiting for transfers between devices  26.9 us (36%)
  Pallas kernels  22.6 us (30%)
  starting transfers between devices  21 us (28%)
  other arithmetic  4.05 us (5%)
    ppermute x9, waiting for transfers between devices, swapped_with(): lax.ppermute(value, axis, [(s, s ^ bit) for s in range(lax.axis_size(axis...  17.2 us
    pallas_call x3, Pallas kernels, late(): pl.pallas_call(late_body, grid=(width // tile,), in_specs=in_specs, out_s...  11.7 us
    ppermute x4, starting transfers between devices, shifted(): lax.ppermute(value, 'seq', [(s, s + steps) for s in range(count - steps)])  11.5 us
    pallas_call x3, Pallas kernels, early(): pl.pallas_call(early_body, grid=(width // tile,), in_specs=[pl.BlockSpec(...  10.9 us
    ppermute x4, waiting for transfers between devices, shifted(): lax.ppermute(value, 'seq', [(s, s + steps) for s in range(count - steps)])  9.71 us
    ppermute x9, starting transfers between devices, swapped_with(): lax.ppermute(value, axis, [(s, s ^ bit) for s in range(lax.axis_size(axis...  9.58 us
    reduce_sum x1, other arithmetic, on_device(): squares = sum_over(jnp.sum(values * values, axis=1, keepdims=True), 'chan')  1.52 us
  transfers between devices with their start and end apart: 13, of which 4 were waited for; matrix products, arithmetic and copies ran while one was open for 1% of the time, Pallas kernels for 24%

commit v1 on v0

--- a/solution.py
+++ b/solution.py
@@ -12,8 +12,9 @@
 BF16 = jnp.bfloat16
 F32 = jnp.float32
 EPS = 1e-06
+SEP = (2,)
 GROUP = 4
-VMEM_LIMIT = 48 * 2**20
+VMEM_LIMIT = 20 * 2**20
 
 
 def split(table):
@@ -63,7 +64,19 @@
     return jnp.where(flag, left[0], right[0]), jnp.where(flag, left[1], right[1])
 
 
-def early_body(core, forward, own, far, side, taps, acc, mid, other):
+def store(ref, value):
+    rows = value[0].shape[0]
+    ref[:rows, :] = value[0]
+    ref[rows:, :] = value[1]
+
+
+def load(ref):
+    rows = ref.shape[0] // 2
+    return ref[:rows, :], ref[rows:, :]
+
+
+def early_body(core, forward, own, far, *rest):
+    *side, taps, total_out, side_out, near_out, swap_out = rest
     rows = own.shape[0]
     table = forward[...]
     first = core[0] == 0
@@ -71,20 +84,18 @@
     h = [g[0]] + [plus(g[j], delayed(*g[j - 1])) for j in range(1, GROUP)] + [delayed(*g[GROUP - 1])]
     total = times(spectrum(table, own[...]), h[0])
     total = plus(total, times(spectrum(table, far[...]), h[4]))
-    total = plus(total, times(spectrum(table, side[...]), pick(first, h[3], h[1])))
-    last = pick(first, h[1], h[3])
-    for ref, value in ((acc, total), (mid, h[2]), (other, last)):
-        ref[:rows, :] = value[0]
-        ref[rows:, :] = value[1]
-
-
-def late_body(forward, back, near, swapped, own, far, gate, scales, acc, mid, other, *rest):
+    store(total_out, total)
+    store(side_out, pick(first, h[3], h[1]))
+    store(near_out, h[2])
+    store(swap_out, pick(first, h[1], h[3]))
+
+
+def late_body(forward, back, side, near, swap, own, far, gate, scales, total_in, h_side, h_near, h_swap, *rest):
     out = rest[-1]
-    rows = own.shape[0]
     table = forward[...]
-    total = (acc[:rows, :], acc[rows:, :])
-    total = plus(total, times(spectrum(table, near[...]), (mid[:rows, :], mid[rows:, :])))
-    total = plus(total, times(spectrum(table, swapped[...]), (other[:rows, :], other[rows:, :])))
+    total = load(total_in)
+    for block, h in ((side, h_side), (near, h_near), (swap, h_swap)):
+        total = plus(total, times(spectrum(table, block[...]), load(h)))
     total = jnp.concatenate(total, 0)
     high = total.astype(BF16)
     low = (total - high.astype(F32)).astype(BF16)
@@ -94,18 +105,32 @@
     out[...] = (gate[...].astype(F32) * mixed).astype(BF16)
 
 
+def squares_body(x, out):
+    values = x[...].astype(F32)
+    total = jnp.sum(values * values, axis=1, keepdims=True)
+    out[...] = jnp.broadcast_to(total, (total.shape[0], total.shape[0])).T[: out.shape[0], :]
+
+
+def normed_body(total_channels, starts, x, squares, *outs):
+    rows = x.shape[0]
+    column = jnp.broadcast_to(squares[0:1, :], (rows, rows)).T[:, 0:1]
+    factor = lax.rsqrt(column / total_channels + EPS)
+    for start, out in zip(starts, outs):
+        out[...] = (x[:, start : start + out.shape[1]].astype(F32) * factor).astype(BF16)
+
+
 def whole(array):
     return pl.BlockSpec(array.shape, lambda i: (0,) * array.ndim)
 
 
-def columns(rows, tile, start=0):
-    return pl.BlockSpec((rows, tile), lambda i: (0, start // tile + i))
+def columns(rows, tile, start=0, block=0):
+    return pl.BlockSpec((rows, tile), lambda i: (block, start // tile + i))
 
 
 PARAMS = pltpu.CompilerParams(vmem_limit_bytes=VMEM_LIMIT)
 
 
-def early(core, forward, own, far, side, long_filter, start, tile):
+def early(core, forward, own, far, long_filter, start, tile):
     rows, width = own.shape
     spec = columns(2 * rows, tile)
     shape = jax.ShapeDtypeStruct((2 * rows, width), F32)
@@ -113,23 +138,23 @@
         early_body,
         grid=(width // tile,),
         in_specs=[pl.BlockSpec(memory_space=pltpu.SMEM), whole(forward)]
-        + [columns(rows, tile)] * 3
+        + [columns(rows, tile)] * 2
         + [columns(GROUP * rows, tile, start)],
-        out_specs=[spec] * 3,
-        out_shape=[shape] * 3,
+        out_specs=[spec] * 4,
+        out_shape=[shape] * 4,
         compiler_params=PARAMS,
-    )(core, forward, own, far, side, long_filter)
-
-
-def late(forward, back, near, swapped, own, far, gate, scales, kept, start, tile, out):
+    )(core, forward, own, far, long_filter)
+
+
+def late(forward, back, side, near, swap, own, far, gate, scales, kept, start, tile, out):
     rows, width = own.shape
-    spec = columns(2 * rows, tile)
-    operands = [forward, back, near, swapped, own, far, gate, scales, *kept]
+    operands = [forward, back, side, near, swap, own, far, gate, scales, *kept]
     in_specs = (
         [whole(forward), whole(back)]
-        + [columns(rows, tile)] * 4
+        + [columns(rows, tile), columns(rows, tile), columns(rows, tile, 0, swap.shape[0] // rows - 1)]
+        + [columns(rows, tile)] * 2
         + [columns(rows, tile, start), columns(2, tile, start)]
-        + [spec] * 3
+        + [columns(2 * rows, tile)] * 4
     )
     aliases = {}
     if out is not None:
@@ -174,26 +199,54 @@
     on_low = place // 2 % 2 == 0
     forward, back = (jnp.asarray(table) for table in tables(rows))
 
-    values = inputs.astype(F32)
-    squares = sum_over(jnp.sum(values * values, axis=1, keepdims=True), "chan")
-    total_channels = channels * lax.axis_size("chan")
-    normed = (values * lax.rsqrt(squares / total_channels + EPS)).astype(BF16)
     scales = jnp.stack([long_filter[-1].astype(F32), skip_scale])
 
     tile = channels // 8
-    widths = [2 * tile, 3 * tile, 3 * tile]
-    starts = [0, 2 * tile, 5 * tile]
-    own = [normed[:, s : s + w] for s, w in zip(starts, widths)]
+    widths = [3 * tile, 3 * tile, 2 * tile]
+    starts = [0, 3 * tile, 6 * tile]
+    squares = pl.pallas_call(
+        squares_body, out_shape=jax.ShapeDtypeStruct((8, rows), F32), compiler_params=PARAMS
+    )(inputs)
+    squares = sum_over(squares, "chan")
+    own = pl.pallas_call(
+        functools.partial(normed_body, channels * lax.axis_size("chan"), starts),
+        out_shape=[jax.ShapeDtypeStruct((rows, w), BF16) for w in widths],
+        compiler_params=PARAMS,
+    )(inputs, squares)
+    own = list(own)
     far = [shifted(block, 4) for block in own]
-    near = [swapped_with(jnp.where(on_low, own[k], far[k]), "seq", 2) for k in range(2)]
-    near.append(shifted(own[2], 2))
-    out = None
+    straight = shifted(own[2], 2)
     core_arg = core.astype(jnp.int32).reshape(1)
-    for k in range(3):
-        side = swapped_with(jnp.where(core == 0, own[k], far[k]), "seq", 1)
-        kept = early(core_arg, forward, own[k], far[k], side, long_filter, starts[k], tile)
-        other = swapped_with(near[k], "seq", 1)
-        out = late(forward, back, near[k], other, own[k], far[k], gating, scales, kept, starts[k], tile, out)
+    tie = lax.optimization_barrier
+
+    def begin(k):
+        return early(core_arg, forward, own[k], far[k], long_filter, starts[k], tile)
+
+    def turn(k):
+        return swapped_with(jnp.where(on_low, own[k], far[k]), "seq", 2)
+
+    def finish(k, near, out):
+        side = jnp.where(core == 0, own[k], far[k])
+        if k in SEP:
+            side = swapped_with(side, "seq", 1)
+            swap = swapped_with(near, "seq", 1)
+        else:
+            side = swap = swapped_with(jnp.concatenate([side, near], 0), "seq", 1)
+        return late(forward, back, side, near, swap, own[k], far[k], gating, scales, kept[k], starts[k], tile, out)
+
+    kept = [None] * 3
+    near = [turn(0), None, straight]
+    kept[0] = begin(0)
+    far[1], kept[0] = tie((far[1], kept[0]))
+    near[1] = turn(1)
+    kept[1] = begin(1)
+    far[2], kept[1], near[0] = tie((far[2], kept[1], near[0]))
+    kept[2] = begin(2)
+    near[2], kept[2] = tie((near[2], kept[2]))
+    out = finish(0, near[0], None)
+    out = finish(2, near[2], out)
+    near[1], out = tie((near[1], out))
+    out = finish(1, near[1], out)
     return out
 
 

time: 75.5 us -> 53 us (0.70)
  waiting for transfers between devices: 26.9 us -> 9.93 us
  Pallas kernels: 22.6 us -> 18.2 us
  local copies, waits for them, and re-layouts: 0.08 us -> 3.45 us
  other arithmetic: 4.05 us -> 1.13 us
  starting transfers between devices: 21 us -> 19.7 us
    ppermute x9 -> x7, waiting for transfers between devices: 17.2 us -> 4.27 us  [swapped_with(): lax.ppermute(value, axis, [(s, s ^ bit) for s in range(lax.axis_size(axis...]
    ppermute x4, waiting for transfers between devices: 9.71 us -> 5.66 us  [shifted(): lax.ppermute(value, 'seq', [(s, s + steps) for s in range(count - steps)])]
    pallas_call x3, Pallas kernels: 10.9 us -> 7.12 us  [early(): pl.pallas_call(early_body, grid=(width // tile,), in_specs=[pl.BlockSpec(...]
    unnamed x12 -> x14, local copies, waits for them, and re-layouts: 0.03 us -> 3.45 us
    ppermute x4, starting transfers between devices: 11.5 us -> 9.18 us  [shifted(): lax.ppermute(value, 'seq', [(s, s + steps) for s in range(count - steps)])]
    reduce_sum x1 -> x0, other arithmetic: 1.52 us -> none  [on_device(): squares = sum_over(jnp.sum(values * values, axis=1, keepdims=True), 'chan')]
    convert_element_type x1 -> x0, other arithmetic: 1.48 us -> none  [on_device(): normed = (values * lax.rsqrt(squares / total_channels + EPS)).astype(BF16)]
    pallas_call x3, Pallas kernels: 11.7 us -> 10.4 us  [late(): pl.pallas_call(late_body, grid=(width // tile,), in_specs=in_specs, out_s...]
  transfers between devices with their start and end apart: 13 -> 11, of which waited for: 4 -> 5; matrix products, arithmetic and copies ran while one was open for 1% -> 2% of each run, Pallas kernels for 24% -> 26%
where the time goes in v1:
time: 53 us; the launch traced here: 52.6 us
  starting transfers between devices  19.7 us (37%)
  Pallas kernels  18.2 us (34%)
  waiting for transfers between devices  9.93 us (19%)
  local copies, waits for them, and re-layouts  3.45 us (7%)
  other arithmetic  1.13 us (2%)
    ppermute x7, starting transfers between devices, swapped_with(): lax.ppermute(value, axis, [(s, s ^ bit) for s in range(lax.axis_size(axis...  10.6 us
    pallas_call x3, Pallas kernels, late(): pl.pallas_call(late_body, grid=(width // tile,), in_specs=in_specs, out_s...  10.4 us
    ppermute x4, starting transfers between devices, shifted(): lax.ppermute(value, 'seq', [(s, s + steps) for s in range(count - steps)])  9.18 us
    pallas_call x3, Pallas kernels, early(): pl.pallas_call(early_body, grid=(width // tile,), in_specs=[pl.BlockSpec(...  7.12 us
    ppermute x4, waiting for transfers between devices, shifted(): lax.ppermute(value, 'seq', [(s, s + steps) for s in range(count - steps)])  5.66 us
    ppermute x7, waiting for transfers between devices, swapped_with(): lax.ppermute(value, axis, [(s, s ^ bit) for s in range(lax.axis_size(axis...  4.27 us
    unnamed x14, local copies, waits for them, and re-layouts  3.45 us
  transfers between devices with their start and end apart: 11, of which 5 were waited for; matrix products, arithmetic and copies ran while one was open for 2% of the time, Pallas kernels for 26%

profile of v1, /device:TPU:17, one launch (start us, length us, event | category | flops | bytes accessed | tf_op | source)
XLA Modules:
  0.0 52.6 jit_solution(5580374464406181405)
XLA Ops:
  0.0 1.2 %copy-done.4 = bf16[128,4096]{1,0:T(8,128)(2,1)S(1)} copy-done((bf16[128,4096]{1,0:T(8,128)(2,1)S(1)}, bf16[128,4096]{1,0:T(8,128)(2,1)}, u32[]{:S(2)}) %copy-start.4) | copy-done | bytes 1048600
  1.2 0.3 shard_map.64
  1.5 1.2 %collective-permute-start = (f32[8,128]{1,0:T(8,128)S(1)}, f32[8,128]{1,0:T(8,128)S(1)}, u32[]{:S(2)}, u32[]{:S(2)}) collective-permute-start(f32[8,128]{1,0:T(8,128)S(1)} %shard_map.64), channel_id=1, source_target_pairs={{0,1},{1,0},{2,3},{3,2},{4,5},{5,4},{6,7},{7,6},{8,9},{9,8},{10,11... | collective-permute-start | bytes 12296 | tf_op jit(solution)/shard_map/ppermute | solution.py:181
  2.8 1.2 %collective-permute-done = f32[8,128]{1,0:T(8,128)S(1)} collective-permute-done((f32[8,128]{1,0:T(8,128)S(1)}, f32[8,128]{1,0:T(8,128)S(1)}, u32[]{:S(2)}, u32[]{:S(2)}) %collective-permute-start) | collective-permute-done | bytes 4128 | tf_op jit(solution)/shard_map/ppermute | solution.py:181
  4.0 0.3 shard_map.65
  4.3 3.2 %collective-permute-start.2 = (bf16[128,1536]{1,0:T(8,128)(2,1)S(1)}, bf16[128,1536]{1,0:T(8,128)(2,1)S(1)}, u32[]{:S(2)}, u32[]{:S(2)}) collective-permute-start(bf16[128,1536]{1,0:T(8,128)(2,1)S(1)} %get-tuple-element.39.own), channel_id=1, source_target_pairs={{0,8},{2,10},{4,12},{6,14},{8,16},{10,18},{12,20},{14,22},{16,24},... | collective-permute-start | bytes 1179656 | tf_op jit(solution)/shard_map/ppermute | solution.py:177
  7.6 1.9 %collective-permute-start.1 = (bf16[128,1536]{1,0:T(8,128)(2,1)S(1)}, bf16[128,1536]{1,0:T(8,128)(2,1)S(1)}, u32[]{:S(2)}, u32[]{:S(2)}) collective-permute-start(bf16[128,1536]{1,0:T(8,128)(2,1)S(1)} %get-tuple-element.38.own), channel_id=1, source_target_pairs={{0,8},{2,10},{4,12},{6,14},{8,16},{10,18},{12,20},{14,22},{16,24},... | collective-permute-start | bytes 1179656 | tf_op jit(solution)/shard_map/ppermute | solution.py:177
  9.5 1.9 %collective-permute-start.4 = (bf16[128,1024]{1,0:T(8,128)(2,1)S(1)}, bf16[128,1024]{1,0:T(8,128)(2,1)S(1)}, u32[]{:S(2)}, u32[]{:S(2)}) collective-permute-start(bf16[128,1024]{1,0:T(8,128)(2,1)S(1)} %get-tuple-element.45.own), channel_id=1, source_target_pairs={{0,8},{2,10},{4,12},{6,14},{8,16},{10,18},{12,20},{14,22},{16,24},... | collective-permute-start | bytes 786440 | tf_op jit(solution)/shard_map/ppermute | solution.py:177
  11.4 3.6 %collective-permute-done.2.far = bf16[128,1536]{1,0:T(8,128)(2,1)S(1)} collective-permute-done((bf16[128,1536]{1,0:T(8,128)(2,1)S(1)}, bf16[128,1536]{1,0:T(8,128)(2,1)S(1)}, u32[]{:S(2)}, u32[]{:S(2)}) %collective-permute-start.2) | collective-permute-done | bytes 393248 | tf_op jit(solution)/shard_map/ppermute | solution.py:177
  15.0 0.1 broadcast_select_fusion.2
  15.1 1.3 %collective-permute-start.5 = (bf16[128,1536]{1,0:T(8,128)(2,1)S(1)}, bf16[128,1536]{1,0:T(8,128)(2,1)S(1)}, u32[]{:S(2)}, u32[]{:S(2)}) collective-permute-start(bf16[128,1536]{1,0:T(8,128)(2,1)S(1)} %get-tuple-element.74), channel_id=1, source_target_pairs={{0,4},{2,6},{4,0},{6,2},{8,12},{10,14},{12,8},{14,10},{16,20},{18,... | collective-permute-start | bytes 1179656 | tf_op jit(solution)/shard_map/ppermute | solution.py:181
  16.4 0.8 %slice_convert_fusion = f32[1,4096]{1,0:T(1,128)S(1)} fusion(bf16[513,4096]{1,0:T(8,128)(2,1)} %rest_0_.5), kind=kLoop, calls=%fused_computation.8 | loop fusion | flops 4096 | bytes 24576 | tf_op jit(solution)/shard_map/convert_element_type | solution.py:202
  17.2 2.1 %collective-permute-start.7 = (bf16[128,1024]{1,0:T(8,128)(2,1)S(1)}, bf16[128,1024]{1,0:T(8,128)(2,1)S(1)}, u32[]{:S(2)}, u32[]{:S(2)}) collective-permute-start(bf16[128,1024]{1,0:T(8,128)(2,1)S(1)} %get-tuple-element.45.own), channel_id=1, source_target_pairs={{0,4},{2,6},{4,8},{6,10},{8,12},{10,14},{12,16},{14,18},{16,20},{1... | collective-permute-start | bytes 786440 | tf_op jit(solution)/shard_map/ppermute | solution.py:177
  19.4 2.2 %copy-done = bf16[513,4096]{1,0:T(8,128)(2,1)S(1)} copy-done((bf16[513,4096]{1,0:T(8,128)(2,1)S(1)}, bf16[513,4096]{1,0:T(8,128)(2,1)}, u32[]{:S(2)}) %copy-start) | copy-done | bytes 4202520
  21.6 2.7 %shard_map.66 = (f32[256,1536]{1,0:T(8,128)S(1)}, f32[256,1536]{1,0:T(8,128)S(1)}, f32[256,1536]{1,0:T(8,128)S(1)}, f32[256,1536]{1,0:T(8,128)S(1)}) custom-call(s32[1]{0:T(128)} %bitcast.core, bf16[256,256]{1,0:T(8,128)(2,1)S(1)} %copy-done.3, bf16[128,1536]{1,0:T(8,128)(2,1)S(1)} %get-tuple-element.39.own, ...), custom_call_target="tpu_custom_call" | custom-call | tf_op jit(solution)/shard_map/pallas_call | solution.py:137
  24.3 2.7 %shard_map.67 = (f32[256,1536]{1,0:T(8,128)S(1)}, f32[256,1536]{1,0:T(8,128)S(1)}, f32[256,1536]{1,0:T(8,128)S(1)}, f32[256,1536]{1,0:T(8,128)S(1)}) custom-call(s32[1]{0:T(128)} %bitcast.core, bf16[256,256]{1,0:T(8,128)(2,1)S(1)} %copy-done.3, bf16[128,1536]{1,0:T(8,128)(2,1)S(1)} %get-tuple-element.38.own, ...), custom_call_target="tpu_custom_call" | custom-call | tf_op jit(solution)/shard_map/pallas_call | solution.py:137
  27.0 2.1 %collective-permute-done.4.far = bf16[128,1024]{1,0:T(8,128)(2,1)S(1)} collective-permute-done((bf16[128,1024]{1,0:T(8,128)(2,1)S(1)}, bf16[128,1024]{1,0:T(8,128)(2,1)S(1)}, u32[]{:S(2)}, u32[]{:S(2)}) %collective-permute-start.4) | collective-permute-done | bytes 262176 | tf_op jit(solution)/shard_map/ppermute | solution.py:177
  29.1 0.1 pad_maximum_fusion
  29.1 3.7 %collective-permute-start.9 = (bf16[256,1536]{1,0:T(8,128)(2,1)S(1)}, bf16[256,1536]{1,0:T(8,128)(2,1)S(1)}, u32[]{:S(2)}, u32[]{:S(2)}) collective-permute-start(bf16[256,1536]{1,0:T(8,128)(2,1)S(1)} %pad_maximum_fusion), channel_id=1, source_target_pairs={{0,2},{2,0},{4,6},{6,4},{8,10},{10,8},{12,14},{14,12},{16,18},{18,... | collective-permute-start | bytes 2359304 | tf_op jit(solution)/shard_map/ppermute | solution.py:181
  32.8 0.1 broadcast_select_fusion.3
  32.8 0.0 copy-start.5
  32.9 2.8 %collective-permute-start.3 = (bf16[128,1536]{1,0:T(8,128)(2,1)S(1)}, bf16[128,1536]{1,0:T(8,128)(2,1)S(1)}, u32[]{:S(2)}, u32[]{:S(2)}) collective-permute-start(bf16[128,1536]{1,0:T(8,128)(2,1)S(1)} %get-tuple-element.72), channel_id=1, source_target_pairs={{0,4},{2,6},{4,0},{6,2},{8,12},{10,14},{12,8},{14,10},{16,20},{18,... | collective-permute-start | bytes 1179656 | tf_op jit(solution)/shard_map/ppermute | solution.py:181
  35.7 1.8 %shard_map.68 = (f32[256,1024]{1,0:T(8,128)S(1)}, f32[256,1024]{1,0:T(8,128)S(1)}, f32[256,1024]{1,0:T(8,128)S(1)}, f32[256,1024]{1,0:T(8,128)S(1)}) custom-call(s32[1]{0:T(128)} %bitcast.core, bf16[256,256]{1,0:T(8,128)(2,1)S(1)} %copy-done.3, bf16[128,1024]{1,0:T(8,128)(2,1)S(1)} %get-tuple-element.45.own, ...), custom_call_target="tpu_custom_call" | custom-call | tf_op jit(solution)/shard_map/pallas_call | solution.py:137
  37.5 1.0 %collective-permute-start.8 = (bf16[128,1024]{1,0:T(8,128)(2,1)S(1)}, bf16[128,1024]{1,0:T(8,128)(2,1)S(1)}, u32[]{:S(2)}, u32[]{:S(2)}) collective-permute-start(bf16[128,1024]{1,0:T(8,128)(2,1)S(1)} %collective-permute-done.7.near), channel_id=1, source_target_pairs={{0,2},{2,0},{4,6},{6,4},{8,10},{10,8},{12,14},{14,12},{16,18},{18,... | collective-permute-start | bytes 786440 | tf_op jit(solution)/shard_map/ppermute | solution.py:181
  38.5 0.1 collective-permute-start.6
  38.7 3.8 %shard_map.69.rest_0_ = bf16[128,4096]{1,0:T(8,128)(2,1)} custom-call(bf16[256,256]{1,0:T(8,128)(2,1)S(1)} %copy-done.3, bf16[128,768]{1,0:T(8,128)(2,1)S(1)} %copy-done.5, bf16[256,1536]{1,0:T(8,128)(2,1)S(1)} %collective-permute-done.9.side.swap, bf16[128,1536]{1,0:T(8,128)(2,1)S(1)} %collective-permute-done.5.near, ...), custom_call_target="tpu_custom_call" | custom-call | tf_op jit(solution)/shard_map/pallas_call | solution.py:164
  42.5 2.8 %shard_map.70.rest_0_ = bf16[128,4096]{1,0:T(8,128)(2,1)} custom-call(bf16[256,256]{1,0:T(8,128)(2,1)S(1)} %copy-done.3, bf16[128,768]{1,0:T(8,128)(2,1)S(1)} %copy-done.5, bf16[128,1024]{1,0:T(8,128)(2,1)S(1)} %collective-permute-done.6.side, bf16[128,1024]{1,0:T(8,128)(2,1)S(1)} %collective-permute-done.7.near, ...), custom_call_target="tpu_custom_call", output_to_operand_aliasing={{}: (13, {})} | custom-call | tf_op jit(solution)/shard_map/pallas_call | solution.py:164
  45.3 1.1 %collective-permute-done.3.near = bf16[128,1536]{1,0:T(8,128)(2,1)S(1)} collective-permute-done((bf16[128,1536]{1,0:T(8,128)(2,1)S(1)}, bf16[128,1536]{1,0:T(8,128)(2,1)S(1)}, u32[]{:S(2)}, u32[]{:S(2)}) %collective-permute-start.3) | collective-permute-done | bytes 393248 | tf_op jit(solution)/shard_map/ppermute | solution.py:181
  46.4 0.1 pad_maximum_fusion.1
  46.4 0.5 collective-permute-start.10
  46.9 1.9 %collective-permute-done.10.side.swap = bf16[256,1536]{1,0:T(8,128)(2,1)S(1)} collective-permute-done((bf16[256,1536]{1,0:T(8,128)(2,1)S(1)}, bf16[256,1536]{1,0:T(8,128)(2,1)S(1)}, u32[]{:S(2)}, u32[]{:S(2)}) %collective-permute-start.10) | collective-permute-done | bytes 786464 | tf_op jit(solution)/shard_map/ppermute | solution.py:181
  48.8 3.8 %shard_map.71 = bf16[128,4096]{1,0:T(8,128)(2,1)} custom-call(bf16[256,256]{1,0:T(8,128)(2,1)S(1)} %copy-done.3, bf16[128,768]{1,0:T(8,128)(2,1)S(1)} %copy-done.5, bf16[256,1536]{1,0:T(8,128)(2,1)S(1)} %collective-permute-done.10.side.swap, bf16[128,1536]{1,0:T(8,128)(2,1)S(1)} %collective-permute-done.3.near, ...), custom_call_target="tpu_custom_call", output_to_operand_aliasing={{}: (13, {})} | custom-call | tf_op jit(solution)/shard_map/pallas_call | solution.py:164
  (20 shorter events, 0.1 us)
Async XLA Ops:
  0.0 1.2 %copy-start.4 = (bf16[128,4096]{1,0:T(8,128)(2,1)S(1)}, bf16[128,4096]{1,0:T(8,128)(2,1)}, u32[]{:S(2)}) copy-start(bf16[128,4096]{1,0:T(8,128)(2,1)} %x.3) | copy-start | bytes 3145732
  1.5 17.8 %copy-start.3 = (bf16[256,256]{1,0:T(8,128)(2,1)S(1)}, bf16[256,256]{1,0:T(8,128)(2,1)}, u32[]{:S(2)}) copy-start(bf16[256,256]{1,0:T(8,128)(2,1)} %constant.39.clone.forward) | copy-start | bytes 393220
  1.5 2.5 %collective-permute-start = (f32[8,128]{1,0:T(8,128)S(1)}, f32[8,128]{1,0:T(8,128)S(1)}, u32[]{:S(2)}, u32[]{:S(2)}) collective-permute-start(f32[8,128]{1,0:T(8,128)S(1)} %shard_map.64), channel_id=1, source_target_pairs={{0,1},{1,0},{2,3},{3,2},{4,5},{5,4},{6,7},{7,6},{8,9},{9,8},{10,11... | collective-permute-start | bytes 12296 | tf_op jit(solution)/shard_map/ppermute | solution.py:181
  4.3 10.7 %collective-permute-start.2 = (bf16[128,1536]{1,0:T(8,128)(2,1)S(1)}, bf16[128,1536]{1,0:T(8,128)(2,1)S(1)}, u32[]{:S(2)}, u32[]{:S(2)}) collective-permute-start(bf16[128,1536]{1,0:T(8,128)(2,1)S(1)} %get-tuple-element.39.own), channel_id=1, source_target_pairs={{0,8},{2,10},{4,12},{6,14},{8,16},{10,18},{12,20},{14,22},{16,24},... | collective-permute-start | bytes 1179656 | tf_op jit(solution)/shard_map/ppermute | solution.py:177
  7.6 16.7 %collective-permute-start.1 = (bf16[128,1536]{1,0:T(8,128)(2,1)S(1)}, bf16[128,1536]{1,0:T(8,128)(2,1)S(1)}, u32[]{:S(2)}, u32[]{:S(2)}) collective-permute-start(bf16[128,1536]{1,0:T(8,128)(2,1)S(1)} %get-tuple-element.38.own), channel_id=1, source_target_pairs={{0,8},{2,10},{4,12},{6,14},{8,16},{10,18},{12,20},{14,22},{16,24},... | collective-permute-start | bytes 1179656 | tf_op jit(solution)/shard_map/ppermute | solution.py:177
  9.5 19.5 %collective-permute-start.4 = (bf16[128,1024]{1,0:T(8,128)(2,1)S(1)}, bf16[128,1024]{1,0:T(8,128)(2,1)S(1)}, u32[]{:S(2)}, u32[]{:S(2)}) collective-permute-start(bf16[128,1024]{1,0:T(8,128)(2,1)S(1)} %get-tuple-element.45.own), channel_id=1, source_target_pairs={{0,8},{2,10},{4,12},{6,14},{8,16},{10,18},{12,20},{14,22},{16,24},... | collective-permute-start | bytes 786440 | tf_op jit(solution)/shard_map/ppermute | solution.py:177
  15.1 14.0 %collective-permute-start.5 = (bf16[128,1536]{1,0:T(8,128)(2,1)S(1)}, bf16[128,1536]{1,0:T(8,128)(2,1)S(1)}, u32[]{:S(2)}, u32[]{:S(2)}) collective-permute-start(bf16[128,1536]{1,0:T(8,128)(2,1)S(1)} %get-tuple-element.74), channel_id=1, source_target_pairs={{0,4},{2,6},{4,0},{6,2},{8,12},{10,14},{12,8},{14,10},{16,20},{18,... | collective-permute-start | bytes 1179656 | tf_op jit(solution)/shard_map/ppermute | solution.py:181
  17.2 20.2 %collective-permute-start.7 = (bf16[128,1024]{1,0:T(8,128)(2,1)S(1)}, bf16[128,1024]{1,0:T(8,128)(2,1)S(1)}, u32[]{:S(2)}, u32[]{:S(2)}) collective-permute-start(bf16[128,1024]{1,0:T(8,128)(2,1)S(1)} %get-tuple-element.45.own), channel_id=1, source_target_pairs={{0,4},{2,6},{4,8},{6,10},{8,12},{10,14},{12,16},{14,18},{16,20},{1... | collective-permute-start | bytes 786440 | tf_op jit(solution)/shard_map/ppermute | solution.py:177
  19.4 2.2 %copy-start = (bf16[513,4096]{1,0:T(8,128)(2,1)S(1)}, bf16[513,4096]{1,0:T(8,128)(2,1)}, u32[]{:S(2)}) copy-start(bf16[513,4096]{1,0:T(8,128)(2,1)} %rest_0_.5) | copy-start | bytes 12607492
  21.6 2.7 %copy-start.1 = (bf16[513,4096]{1,0:T(8,128)(2,1)S(1)}, bf16[513,4096]{1,0:T(8,128)(2,1)}, u32[]{:S(2)}) copy-start(bf16[513,4096]{1,0:T(8,128)(2,1)} %rest_0_.5) | copy-start | bytes 12607492
  29.1 9.5 %collective-permute-start.9 = (bf16[256,1536]{1,0:T(8,128)(2,1)S(1)}, bf16[256,1536]{1,0:T(8,128)(2,1)S(1)}, u32[]{:S(2)}, u32[]{:S(2)}) collective-permute-start(bf16[256,1536]{1,0:T(8,128)(2,1)S(1)} %pad_maximum_fusion), channel_id=1, source_target_pairs={{0,2},{2,0},{4,6},{6,4},{8,10},{10,8},{12,14},{14,12},{16,18},{18,... | collective-permute-start | bytes 2359304 | tf_op jit(solution)/shard_map/ppermute | solution.py:181
  32.8 5.8 %copy-start.6 = (f32[4096]{0:T(1024)S(1)}, f32[4096]{0:T(1024)}, u32[]{:S(2)}) copy-start(f32[4096]{0:T(1024)} %param.9) | copy-start | bytes 49156
  32.8 5.8 %copy-start.5 = (bf16[128,768]{1,0:T(8,128)(2,1)S(1)}, bf16[128,768]{1,0:T(8,128)(2,1)}, u32[]{:S(2)}) copy-start(bf16[128,768]{1,0:T(8,128)(2,1)} %constant.40.clone.back) | copy-start | bytes 589828
  32.9 13.5 %collective-permute-start.3 = (bf16[128,1536]{1,0:T(8,128)(2,1)S(1)}, bf16[128,1536]{1,0:T(8,128)(2,1)S(1)}, u32[]{:S(2)}, u32[]{:S(2)}) collective-permute-start(bf16[128,1536]{1,0:T(8,128)(2,1)S(1)} %get-tuple-element.72), channel_id=1, source_target_pairs={{0,4},{2,6},{4,0},{6,2},{8,12},{10,14},{12,8},{14,10},{16,20},{18,... | collective-permute-start | bytes 1179656 | tf_op jit(solution)/shard_map/ppermute | solution.py:181
  35.7 3.0 %copy-start.2 = (bf16[128,4096]{1,0:T(8,128)(2,1)S(1)}, bf16[128,4096]{1,0:T(8,128)(2,1)}, u32[]{:S(2)}) copy-start(bf16[128,4096]{1,0:T(8,128)(2,1)} %gate.5) | copy-start | bytes 3145732
  37.5 5.0 %collective-permute-start.8 = (bf16[128,1024]{1,0:T(8,128)(2,1)S(1)}, bf16[128,1024]{1,0:T(8,128)(2,1)S(1)}, u32[]{:S(2)}, u32[]{:S(2)}) collective-permute-start(bf16[128,1024]{1,0:T(8,128)(2,1)S(1)} %collective-permute-done.7.near), channel_id=1, source_target_pairs={{0,2},{2,0},{4,6},{6,4},{8,10},{10,8},{12,14},{14,12},{16,18},{18,... | collective-permute-start | bytes 786440 | tf_op jit(solution)/shard_map/ppermute | solution.py:181
  38.5 4.0 %collective-permute-start.6 = (bf16[128,1024]{1,0:T(8,128)(2,1)S(1)}, bf16[128,1024]{1,0:T(8,128)(2,1)S(1)}, u32[]{:S(2)}, u32[]{:S(2)}) collective-permute-start(bf16[128,1024]{1,0:T(8,128)(2,1)S(1)} %broadcast_select_fusion.4), channel_id=1, source_target_pairs={{0,2},{2,0},{4,6},{6,4},{8,10},{10,8},{12,14},{14,12},{16,18},{18,... | collective-permute-start | bytes 786440 | tf_op jit(solution)/shard_map/ppermute | solution.py:181
  46.4 2.4 %collective-permute-start.10 = (bf16[256,1536]{1,0:T(8,128)(2,1)S(1)}, bf16[256,1536]{1,0:T(8,128)(2,1)S(1)}, u32[]{:S(2)}, u32[]{:S(2)}) collective-permute-start(bf16[256,1536]{1,0:T(8,128)(2,1)S(1)} %pad_maximum_fusion.1), channel_id=1, source_target_pairs={{0,2},{2,0},{4,6},{6,4},{8,10},{10,8},{12,14},{14,12},{16,18},{18,... | collective-permute-start | bytes 2359304 | tf_op jit(solution)/shard_map/ppermute | solution.py:181

commit v2 on v0

v2 whole, which is shorter than its diff:
```python
import functools

import jax
import jax.numpy as jnp
import ml_dtypes
import numpy as np
from jax import lax
from jax.experimental import pallas as pl
from jax.experimental.pallas import tpu as pltpu
from jax.sharding import PartitionSpec as P

BF16 = jnp.bfloat16
F32 = jnp.float32
EPS = 1e-06
CFG = dict(tile=256, cuts=(6, 6), g=1, hk=1, t=0, w=0, p=0, s=1, f=1)
GROUP = 4
LANES = 128
PARTS = 3
PARAMS = pltpu.CompilerParams(vmem_limit_bytes=24 * 2**20)
SMEM = pl.BlockSpec(memory_space=pltpu.SMEM)
VMEM = pl.BlockSpec(memory_space=pltpu.VMEM)
HBM = pl.BlockSpec(memory_space=pltpu.HBM)


def split(table):
    high = table.astype(ml_dtypes.bfloat16)
    low = (table - high.astype(np.float64)).astype(ml_dtypes.bfloat16)
    return high, low


def tables(rows):
    index = np.concatenate([np.arange(0, rows, 2), np.arange(1, rows, 2)])
    turns = (index + 0.5)[:, None] * np.arange(rows)[None, :] / (2 * rows)
    angle = 2 * np.pi * turns
    forward = np.concatenate([np.cos(angle), -np.sin(angle)], 0)
    back = np.concatenate([np.cos(angle), -np.sin(angle)], 0).T / rows
    f_high, f_low = split(forward)
    b_high, b_low = split(back)
    return np.concatenate([f_high, f_low], 1), np.concatenate([b_high, b_low, b_high], 1)


def dot(left, right):
    return jnp.dot(left, right, preferred_element_type=F32)


def spectrum(table, block):
    both = dot(table, jnp.concatenate([block, block], 0))
    half = both.shape[0] // 2
    return both[:half], both[half:]


def delayed(real, imag):
    half = real.shape[0] // 2
    return (
        jnp.concatenate([-imag[:half], imag[half:]], 0),
        jnp.concatenate([real[:half], -real[half:]], 0),
    )


def plus(left, right):
    return left[0] + right[0], left[1] + right[1]


def times(left, right):
    return left[0] * right[0] - left[1] * right[1], left[0] * right[1] + left[1] * right[0]


def store(ref, part, value):
    rows = value[0].shape[0]
    ref[:rows, part] = value[0]
    ref[rows:, part] = value[1]


def load(ref, part):
    rows = ref.shape[0] // 2
    return ref[:rows, part], ref[rows:, part]


def front_body(core, x, out, mine, theirs, sems):
    rows = x.shape[0]
    half = mine.shape[1]
    pieces = sems.shape[1]
    width = half // pieces

    def piece(j, k):
        side = core[0] if j == 1 else 1 - core[0]
        source = x.at[:, pl.ds(pl.multiple_of(side * half + k * width, LANES), width)]
        return pltpu.make_async_copy(source, (theirs, mine)[j].at[:, pl.ds(k * width, width)], sems.at[j, k])

    for j in range(2):
        for k in range(pieces):
            piece(j, k).start()
    total = jnp.zeros((rows, 1), F32)
    for j in range(2):
        for k in range(pieces):
            piece(j, k).wait()
            values = (theirs, mine)[j][:, k * width : (k + 1) * width].astype(F32)
            total = total + jnp.sum(values * values, axis=1, keepdims=True)
    out[...] = jnp.broadcast_to(total, (rows, rows)).T[: out.shape[0], :]


def gather_body(start, core, mine, given, out):
    rows, width = mine.shape[0], out.shape[1]
    for which in range(2):

        @pl.when(core[0] == which)
        def _():
            out[which * rows : (which + 1) * rows, :] = mine[:, start : start + width]
            out[(1 - which) * rows : (2 - which) * rows, :] = given[:, start : start + width]


def column_of(squares):
    rows = squares.shape[1]
    return jnp.broadcast_to(squares[0:1, :], (rows, rows)).T[:, 0:1]


def pack_body(total_channels, start, core, mine, given, squares, given_squares, out):
    rows = mine.shape[0]
    lane = lax.broadcasted_iota(jnp.int32, (rows, LANES), 1)
    columns = [column_of(squares), column_of(given_squares)]
    factors = [lax.rsqrt(column / total_channels + EPS) for column in columns]
    tails = []
    for left in columns:
        tail = jnp.zeros((rows, LANES), F32)
        for k in range(PARTS):
            piece = left.astype(BF16).astype(F32)
            left = left - piece
            tail = jnp.where(lane == k, piece, tail)
        tails.append(tail.astype(BF16))
    width = out.shape[1] - LANES
    for which in range(2):

        @pl.when(core[0] == which)
        def _():
            for block, factor, tail, place in zip((mine, given), factors, tails, (which, 1 - which)):
                there = slice(place * rows, (place + 1) * rows)
                out[there, :width] = (block[:, start : start + width].astype(F32) * factor).astype(BF16)
                out[there, width:] = tail


def spectra_body(tile, core, forward, taps, *rest):
    *outs, held, sems = rest
    rows = forward.shape[1] // 2
    table = forward[...]
    half = outs[0].shape[1]
    count = half // tile
    first = core[0] * half

    def fetch(k):
        source = taps.at[pl.ds(0, GROUP * rows), pl.ds(pl.multiple_of(first + k * tile, LANES), tile)]
        return pltpu.make_async_copy(source, held.at[k], sems.at[k])

    for k in range(count):
        fetch(k).start()
    for k in range(count):
        part = slice(k * tile, (k + 1) * tile)
        fetch(k).wait()
        before = None
        for j in range(GROUP):
            now = spectrum(table, held[k, j * rows : (j + 1) * rows, :])
            store(outs[j], part, now if before is None else plus(now, delayed(*before)))
            before = now
        store(outs[GROUP], part, delayed(*before))


def near_terms(near0, near1, sums, h, part):
    h1, h2, h3 = (load(h[j], part) for j in (1, 2, 3))
    sum0 = plus(sums[0], plus(times(near1, h1), times(near0, h2)))
    return sum0, plus(sums[1], plus(times(near1, h2), times(near0, h3)))


def far_terms(far0, far1, sums, h, part):
    h3, h4 = load(h[3], part), load(h[4], part)
    sum0 = plus(sums[0], plus(times(far1, h3), times(far0, h4)))
    return sum0, plus(sums[1], times(far1, h4))


def blocks(total_channels, block, part, packed):
    rows = block.shape[0] // 2
    halves = [block[j * rows : (j + 1) * rows, part] for j in range(2)]
    if packed is None:
        return halves
    begin = packed.shape[1] - LANES
    sums = sum(packed[:, begin + k : begin + k + 1].astype(F32) for k in range(PARTS))
    factor = lax.rsqrt(sums / total_channels + EPS)
    return [(half.astype(F32) * factor[j * rows : (j + 1) * rows]).astype(BF16) for j, half in enumerate(halves)]


def first_body(total_channels, tile, start, raw, forward, own, far, *rest):
    packed = rest[:2] if raw else (None, None)
    *h, sum0_out, sum1_out = rest[2:] if raw else rest
    table = forward[...]
    for k in range(sum0_out.shape[1] // tile):
        part = slice(k * tile, (k + 1) * tile)
        wide = slice(start + k * tile, start + (k + 1) * tile)
        own0, own1 = (spectrum(table, b) for b in blocks(total_channels, own, part, packed[0]))
        far0, far1 = (spectrum(table, b) for b in blocks(total_channels, far, part, packed[1]))
        same, next_ = load(h[0], wide), load(h[1], wide)
        sums = times(own0, same), plus(times(own1, same), times(own0, next_))
        sums = far_terms(far0, far1, sums, h, wide)
        store(sum0_out, part, sums[0])
        store(sum1_out, part, sums[1])


def second_body(total_channels, tile, start, raw, core, forward, back, own, far, near, *rest):
    packed = rest[:3] if raw else (None, None, None)
    last, skip, gate, given_gate, sum0, sum1, *h, own_out, given_out = rest[3:] if raw else rest
    half = gate.shape[1] // 2
    table = forward[...]
    inverse = back[...]
    first = core[0] * half + start

    def restored(total):
        total = jnp.concatenate(total, 0)
        high = total.astype(BF16)
        low = (total - high.astype(F32)).astype(BF16)
        return dot(inverse, jnp.concatenate([high, high, low], 0))

    for k in range(own_out.shape[1] // tile):
        part = slice(k * tile, (k + 1) * tile)
        local = slice(start + k * tile, start + (k + 1) * tile)
        wide = pl.ds(pl.multiple_of(first + k * tile, LANES), tile)
        near0, near1 = (spectrum(table, b) for b in blocks(total_channels, near, part, packed[2]))
        sums = near_terms(near0, near1, (load(sum0, part), load(sum1, part)), h, local)
        here, there = blocks(total_channels, own, part, packed[0]), blocks(total_channels, far, part, packed[1])
        values = []
        for j in range(2):
            value = restored(sums[j]) + last[:, wide] * there[j].astype(F32)
            values.append(value + skip[:, wide] * here[j].astype(F32))
        mine = jnp.where(core[0] == 0, values[0], values[1])
        other = jnp.where(core[0] == 0, values[1], values[0])
        own_out[:, part] = (gate[:, wide].astype(F32) * mine).astype(BF16)
        given_out[:, part] = (given_gate[:, wide].astype(F32) * other).astype(BF16)


def merge_body(starts, core, *rest):
    *parts, out, sems = rest
    half = out.shape[1] // 2
    count = len(starts)

    def move(k):
        side = core[0] if k < count else 1 - core[0]
        begin = pl.multiple_of(side * half + starts[k % count], LANES)
        return pltpu.make_async_copy(parts[k], out.at[:, pl.ds(begin, parts[k].shape[1])], sems.at[k])

    for k in range(2 * count):
        move(k).start()
    for k in range(2 * count):
        move(k).wait()


def tile_of(width):
    best = LANES
    for tile in range(LANES, CFG["tile"] + 1, LANES):
        if width % tile == 0:
            best = tile
    return best


def spectra(core, forward, taps, half):
    rows = forward.shape[1] // 2
    tile = tile_of(half)
    return pl.pallas_call(
        functools.partial(spectra_body, tile),
        in_specs=[SMEM, VMEM, HBM],
        out_specs=[VMEM] * (GROUP + 1),
        out_shape=[jax.ShapeDtypeStruct((2 * rows, half), F32)] * (GROUP + 1),
        scratch_shapes=[
            pltpu.VMEM((half // tile, GROUP * rows, tile), BF16),
            pltpu.SemaphoreType.DMA((half // tile,)),
        ],
        compiler_params=PARAMS,
    )(core, forward, taps)


def first_part(total_channels, forward, blocks, packed, h, start, width):
    operands = [forward, *blocks, *packed, *h]
    return pl.pallas_call(
        functools.partial(first_body, total_channels, tile_of(width), start, bool(packed)),
        in_specs=[VMEM] * len(operands),
        out_specs=[VMEM] * 2,
        out_shape=[jax.ShapeDtypeStruct((blocks[0].shape[0], width), F32)] * 2,
        compiler_params=PARAMS,
    )(*operands)


def second_part(total_channels, core, forward, back, blocks, packed, small, gates, sums, h, start, width):
    shape = jax.ShapeDtypeStruct((blocks[0].shape[0] // 2, width), BF16)
    operands = [core, forward, back, *blocks, *packed, *small, *gates, *sums, *h]
    return pl.pallas_call(
        functools.partial(second_body, total_channels, tile_of(width), start, bool(packed)),
        in_specs=[SMEM] + [VMEM] * (len(operands) - 1),
        out_specs=[VMEM] * 2,
        out_shape=[shape] * 2,
        compiler_params=PARAMS,
    )(*operands)


def shifted(value, steps):
    count = lax.axis_size("seq")
    return lax.ppermute(value, "seq", [(s, s + steps) for s in range(count - steps)])


def swapped_with(value, axis, bit):
    return lax.ppermute(value, axis, [(s, s ^ bit) for s in range(lax.axis_size(axis))])


def sum_over(value, axis):
    count = lax.axis_size(axis)
    if count & (count - 1):
        return lax.psum(value, axis)
    bit = 1
    while bit < count:
        value = value + swapped_with(value, axis, bit)
        bit *= 2
    return value


def on_device(inputs, gating, long_filter, skip_scale):
    rows, channels = inputs.shape
    half = channels // 2
    place = lax.axis_index("seq")
    core = place % 2
    on_low = place // 2 % 2 == 0
    core_arg = core.astype(jnp.int32).reshape(1)
    forward, back = (jnp.asarray(table) for table in tables(rows))
    tie = lax.optimization_barrier

    units = half // LANES
    cuts = [max(1, units * c // 16) for c in CFG["cuts"]]
    cuts.append(units - sum(cuts))
    cuts = [c * LANES for c in cuts]
    starts = [sum(cuts[:k]) for k in range(len(cuts))]

    inputs = pltpu.with_memory_space_constraint(inputs, pltpu.HBM)
    squares, mine, theirs = pl.pallas_call(
        front_body,
        in_specs=[SMEM, HBM],
        out_specs=[VMEM] * 3,
        out_shape=[jax.ShapeDtypeStruct((8, rows), F32)] + [jax.ShapeDtypeStruct((rows, half), BF16)] * 2,
        scratch_shapes=[pltpu.SemaphoreType.DMA((2, 2))],
        compiler_params=PARAMS,
    )(core_arg, inputs)
    given = swapped_with(theirs, "seq", 1)
    total_channels = channels * lax.axis_size("chan")

    def gathered(k, mine):
        return pl.pallas_call(
            functools.partial(gather_body, starts[k]),
            in_specs=[SMEM, VMEM, VMEM],
            out_specs=VMEM,
            out_shape=jax.ShapeDtypeStruct((2 * rows, cuts[k]), BF16),
            compiler_params=PARAMS,
        )(core_arg, mine, given)

    own = [None, None, gathered(2, mine)]
    straight = shifted(own[2], 2)
    if CFG["t"] == 2:
        squares, own[2] = tie((squares, own[2]))
    squares = sum_over(squares, "chan")
    if CFG["t"] >= 1:
        mine, squares = tie((mine, squares))
    own[0] = gathered(0, mine)
    given_squares = swapped_with(squares, "seq", 1)
    if CFG["p"]:
        given_squares, own[0] = tie((given_squares, own[0]))
    own[1] = pl.pallas_call(
        functools.partial(pack_body, total_channels, starts[1]),
        in_specs=[SMEM] + [VMEM] * 4,
        out_specs=VMEM,
        out_shape=jax.ShapeDtypeStruct((2 * rows, cuts[1] + LANES), BF16),
        compiler_params=PARAMS,
    )(core_arg, mine, given, squares, given_squares)
    if CFG["w"]:
        own[2], own[1] = tie((own[2], own[1]))
    far = [shifted(block, 4) for block in own]

    last = long_filter[GROUP * rows :].astype(F32)
    skip = skip_scale[None, :]
    taps = pltpu.with_memory_space_constraint(long_filter, pltpu.HBM)

    def turned(k):
        return swapped_with(jnp.where(on_low, own[k], far[k]), "seq", 2)

    far[0], own[1] = tie((far[0], own[1]))
    if CFG["s"]:
        far[0], straight = tie((far[0], straight))
    near = [turned(0), None, straight]
    if CFG["hk"] == 1:
        taps, far[0] = tie((taps, far[0]))
    h = spectra(core_arg, forward, taps, half)
    if CFG["hk"] == 1:
        far[1], h = tie((far[1], h))
    sent = jnp.where(on_low, own[1], far[1])
    near_rider = swapped_with(sent[:, cuts[1] :], "seq", 2)
    near[1] = swapped_with(sent[:, : cuts[1]], "seq", 2)
    if CFG["g"] == 1:
        gating, far[0] = tie((gating, far[0]))
    if CFG["g"] == 2:
        gating, far[1] = tie((gating, far[1]))
    if CFG["g"] == 3:
        gating, far[2] = tie((gating, far[2]))
    given_gate = swapped_with(gating, "seq", 1)
    if CFG["f"] == 0:
        far[0], far[1], far[2] = tie((far[0], far[1], far[2]))
    sums, made = [None] * 3, [None] * 3
    for k in range(3):
        packed = () if k == 1 else (own[1], far[1])
        sums[k] = first_part(total_channels, forward, (own[k], far[k]), packed, h, starts[k], cuts[k])
        if k < 2:
            far[k + 1], sums[k] = tie((far[k + 1], sums[k]))
    near[0], near[2], near_rider, sums[2] = tie((near[0], near[2], near_rider, sums[2]))
    order = (0, 2, 1)
    for j, k in enumerate(order):
        packed = () if k == 1 else (own[1], far[1], near_rider)
        made[k] = second_part(
            total_channels, core_arg, forward, back, (own[k], far[k], near[k]), packed,
            (last, skip), (gating, given_gate), sums[k], h, starts[k], cuts[k],
        )
        if j < 2:
            follow = order[j + 1]
            near[follow], made[k] = tie((near[follow], made[k]))
    parts = [swapped_with(part, "seq", 1) for _, part in made]
    return pl.pallas_call(
        functools.partial(merge_body, starts),
        in_specs=[SMEM] + [VMEM] * (2 * len(cuts)),
        out_specs=HBM,
        out_shape=jax.ShapeDtypeStruct(gating.shape, BF16),
        scratch_shapes=[pltpu.SemaphoreType.DMA((2 * len(cuts),))],
        compiler_params=PARAMS,
    )(core_arg, *[mine for mine, _ in made], *parts)


def solution(mesh):
    in_specs = (P("seq", "chan"), P("seq", "chan"), P(None, "chan"), P("chan"))
    out_specs = P("seq", "chan")
    return jax.shard_map(
        on_device, mesh=mesh, in_specs=in_specs, out_specs=out_specs, check_vma=False
    )
```

time: 75.5 us -> 50.1 us (0.66)
  waiting for transfers between devices: 26.9 us -> 9.76 us
  Pallas kernels: 22.6 us -> 16 us
  other arithmetic: 4.05 us -> 0.95 us
  starting transfers between devices: 21 us -> 22.6 us
    ppermute x9 -> x10, waiting for transfers between devices: 17.2 us -> 5.81 us  [swapped_with(): lax.ppermute(value, axis, [(s, s ^ bit) for s in range(lax.axis_size(axis...]
    pallas_call x6 -> x12, Pallas kernels: 22.6 us -> 16 us  [the longest x3 5.25 us: second_part(): pl.pallas_call(functools.partial(second_body, total_channels, tile_of(wid...]
    ppermute x4, waiting for transfers between devices: 9.71 us -> 3.95 us  [shifted(): lax.ppermute(value, 'seq', [(s, s + steps) for s in range(count - steps)])]
    ppermute x9 -> x10, starting transfers between devices: 9.58 us -> 12.3 us  [swapped_with(): lax.ppermute(value, axis, [(s, s ^ bit) for s in range(lax.axis_size(axis...]
    reduce_sum x1 -> x0, other arithmetic: 1.52 us -> none  [on_device(): squares = sum_over(jnp.sum(values * values, axis=1, keepdims=True), 'chan')]
    convert_element_type x2 -> x1, other arithmetic: 2.34 us -> 0.85 us  [on_device(): last = long_filter[GROUP * rows:].astype(F32)]
    ppermute x4, starting transfers between devices: 11.5 us -> 10.3 us  [shifted(): lax.ppermute(value, 'seq', [(s, s + steps) for s in range(count - steps)])]
  transfers between devices with their start and end apart: 13 -> 14, of which waited for: 4 -> 7; matrix products, arithmetic and copies ran while one was open for 1% -> 2% of each run, Pallas kernels for 24% -> 24%
where the time goes in v2:
time: 50.1 us; the launch traced here: 49.7 us
  starting transfers between devices  22.6 us (45%)
  Pallas kernels  16 us (32%)
  waiting for transfers between devices  9.76 us (19%)
  other arithmetic  0.95 us (2%)
    ppermute x10, starting transfers between devices, swapped_with(): lax.ppermute(value, axis, [(s, s ^ bit) for s in range(lax.axis_size(axis...  12.3 us
    ppermute x4, starting transfers between devices, shifted(): lax.ppermute(value, 'seq', [(s, s + steps) for s in range(count - steps)])  10.3 us
    ppermute x10, waiting for transfers between devices, swapped_with(): lax.ppermute(value, axis, [(s, s ^ bit) for s in range(lax.axis_size(axis...  5.81 us
    pallas_call x3, Pallas kernels, second_part(): pl.pallas_call(functools.partial(second_body, total_channels, tile_of(wid...  5.25 us
    pallas_call x3, Pallas kernels, first_part(): pl.pallas_call(functools.partial(first_body, total_channels, tile_of(widt...  4.29 us
    ppermute x4, waiting for transfers between devices, shifted(): lax.ppermute(value, 'seq', [(s, s + steps) for s in range(count - steps)])  3.95 us
    pallas_call x1, Pallas kernels, spectra(): pl.pallas_call(functools.partial(spectra_body, tile), in_specs=[SMEM, VME...  3.56 us
    pallas_call x1, Pallas kernels, on_device(): pl.pallas_call(front_body, in_specs=[SMEM, HBM], out_specs=[VMEM] * 3, ou...  1.54 us
  transfers between devices with their start and end apart: 14, of which 7 were waited for; matrix products, arithmetic and copies ran while one was open for 2% of the time, Pallas kernels for 24%

profile of v2, /device:TPU:17, one launch (start us, length us, event | category | flops | bytes accessed | tf_op | source)
XLA Modules:
  0.0 49.7 jit_solution(3873649202458535080)
XLA Ops:
  0.0 1.5 %shard_map.64 = (f32[8,128]{1,0:T(8,128)S(1)}, bf16[128,2048]{1,0:T(8,128)(2,1)S(1)}, bf16[128,2048]{1,0:T(8,128)(2,1)S(1)}) custom-call(s32[1]{0:T(128)} %bitcast.core, bf16[128,4096]{1,0:T(8,128)(2,1)} %x.1), custom_call_target="tpu_custom_call" | custom-call | tf_op jit(solution)/shard_map/pallas_call | solution.py:336
  1.5 0.7 %collective-permute-start = (bf16[128,2048]{1,0:T(8,128)(2,1)S(1)}, bf16[128,2048]{1,0:T(8,128)(2,1)S(1)}, u32[]{:S(2)}, u32[]{:S(2)}) collective-permute-start(bf16[128,2048]{1,0:T(8,128)(2,1)S(1)} %get-tuple-element.57), channel_id=1, source_target_pairs={{0,2},{2,0},{4,6},{6,4},{8,10},{10,8},{12,14},{14,12},{16,18},{18,... | collective-permute-start | bytes 1572872 | tf_op jit(solution)/shard_map/ppermute | solution.py:305
  2.3 1.5 %collective-permute-done.given = bf16[128,2048]{1,0:T(8,128)(2,1)S(1)} collective-permute-done((bf16[128,2048]{1,0:T(8,128)(2,1)S(1)}, bf16[128,2048]{1,0:T(8,128)(2,1)S(1)}, u32[]{:S(2)}, u32[]{:S(2)}) %collective-permute-start) | collective-permute-done | bytes 524320 | tf_op jit(solution)/shard_map/ppermute | solution.py:305
  3.9 3.3 %collective-permute-start.1 = (bf16[256,768]{1,0:T(8,128)(2,1)S(1)}, bf16[256,768]{1,0:T(8,128)(2,1)S(1)}, u32[]{:S(2)}, u32[]{:S(2)}) collective-permute-start(bf16[256,768]{1,0:T(8,128)(2,1)S(1)} %shard_map.65.own), channel_id=1, source_target_pairs={{0,8},{2,10},{4,12},{6,14},{8,16},{10,18},{12,20},{14,22},{16,24},... | collective-permute-start | bytes 1179656 | tf_op jit(solution)/shard_map/ppermute | solution.py:301
  7.3 3.1 %collective-permute-start.4 = (bf16[256,512]{1,0:T(8,128)(2,1)S(1)}, bf16[256,512]{1,0:T(8,128)(2,1)S(1)}, u32[]{:S(2)}, u32[]{:S(2)}) collective-permute-start(bf16[256,512]{1,0:T(8,128)(2,1)S(1)} %shard_map.67.own), channel_id=1, source_target_pairs={{0,4},{2,6},{4,8},{6,10},{8,12},{10,14},{12,16},{14,18},{16,20},{1... | collective-permute-start | bytes 786440 | tf_op jit(solution)/shard_map/ppermute | solution.py:301
  10.4 1.3 %collective-permute-start.2 = (f32[8,128]{1,0:T(8,128)S(1)}, f32[8,128]{1,0:T(8,128)S(1)}, u32[]{:S(2)}, u32[]{:S(2)}) collective-permute-start(f32[8,128]{1,0:T(8,128)S(1)} %get-tuple-element.58), channel_id=1, source_target_pairs={{0,1},{1,0},{2,3},{3,2},{4,5},{5,4},{6,7},{7,6},{8,9},{9,8},{10,11... | collective-permute-start | bytes 12296 | tf_op jit(solution)/shard_map/ppermute | solution.py:305
  11.7 1.5 %collective-permute-done.2 = f32[8,128]{1,0:T(8,128)S(1)} collective-permute-done((f32[8,128]{1,0:T(8,128)S(1)}, f32[8,128]{1,0:T(8,128)S(1)}, u32[]{:S(2)}, u32[]{:S(2)}) %collective-permute-start.2) | collective-permute-done | bytes 4128 | tf_op jit(solution)/shard_map/ppermute | solution.py:305
  13.2 1.8 %collective-permute-start.3 = (f32[8,128]{1,0:T(8,128)S(1)}, f32[8,128]{1,0:T(8,128)S(1)}, u32[]{:S(2)}, u32[]{:S(2)}) collective-permute-start(f32[8,128]{1,0:T(8,128)S(1)} %add.13.squares), channel_id=1, source_target_pairs={{0,2},{2,0},{4,6},{6,4},{8,10},{10,8},{12,14},{14,12},{16,18},{18,... | collective-permute-start | bytes 12296 | tf_op jit(solution)/shard_map/ppermute | solution.py:305
  15.0 0.8 %collective-permute-done.3.given_squares = f32[8,128]{1,0:T(8,128)S(1)} collective-permute-done((f32[8,128]{1,0:T(8,128)S(1)}, f32[8,128]{1,0:T(8,128)S(1)}, u32[]{:S(2)}, u32[]{:S(2)}) %collective-permute-start.3) | collective-permute-done | bytes 4128 | tf_op jit(solution)/shard_map/ppermute | solution.py:305
  15.9 0.3 shard_map.66.rest_0_.own
  16.2 1.9 %collective-permute-start.6 = (bf16[256,896]{1,0:T(8,128)(2,1)S(1)}, bf16[256,896]{1,0:T(8,128)(2,1)S(1)}, u32[]{:S(2)}, u32[]{:S(2)}) collective-permute-start(bf16[256,896]{1,0:T(8,128)(2,1)S(1)} %shard_map.66.rest_0_.own), channel_id=1, source_target_pairs={{0,8},{2,10},{4,12},{6,14},{8,16},{10,18},{12,20},{14,22},{16,24},... | collective-permute-start | bytes 1376264 | tf_op jit(solution)/shard_map/ppermute | solution.py:301
  18.2 1.9 %collective-permute-start.8 = (bf16[256,512]{1,0:T(8,128)(2,1)S(1)}, bf16[256,512]{1,0:T(8,128)(2,1)S(1)}, u32[]{:S(2)}, u32[]{:S(2)}) collective-permute-start(bf16[256,512]{1,0:T(8,128)(2,1)S(1)} %shard_map.67.own), channel_id=1, source_target_pairs={{0,8},{2,10},{4,12},{6,14},{8,16},{10,18},{12,20},{14,22},{16,24},... | collective-permute-start | bytes 786440 | tf_op jit(solution)/shard_map/ppermute | solution.py:301
  20.1 2.7 %collective-permute-done.4.near = bf16[256,512]{1,0:T(8,128)(2,1)S(1)} collective-permute-done((bf16[256,512]{1,0:T(8,128)(2,1)S(1)}, bf16[256,512]{1,0:T(8,128)(2,1)S(1)}, u32[]{:S(2)}, u32[]{:S(2)}) %collective-permute-start.4) | collective-permute-done | bytes 262176 | tf_op jit(solution)/shard_map/ppermute | solution.py:301
  22.8 0.1 collective-permute-start.5
  22.9 2.1 %collective-permute-start.9 = (bf16[128,4096]{1,0:T(8,128)(2,1)S(1)}, bf16[128,4096]{1,0:T(8,128)(2,1)S(1)}, u32[]{:S(2)}, u32[]{:S(2)}) collective-permute-start(bf16[128,4096]{1,0:T(8,128)(2,1)S(1)} %copy-done), channel_id=1, source_target_pairs={{0,2},{2,0},{4,6},{6,4},{8,10},{10,8},{12,14},{14,12},{16,18},{18,... | collective-permute-start | bytes 3145736 | tf_op jit(solution)/shard_map/ppermute | solution.py:305
  25.0 3.6 %shard_map.68 = (f32[256,2048]{1,0:T(8,128)S(1)}, f32[256,2048]{1,0:T(8,128)S(1)}, f32[256,2048]{1,0:T(8,128)S(1)}, f32[256,2048]{1,0:T(8,128)S(1)}, f32[256,2048]{1,0:T(8,128)S(1)}) custom-call(s32[1]{0:T(128)} %bitcast.core, bf16[256,256]{1,0:T(8,128)(2,1)S(1)} %copy-done.1, bf16[513,4096]{1,0:T(8,128)(2,1)} %taps), custom_call_target="tpu_custom_call" | custom-call | tf_op jit(solution)/shard_map/pallas_call | solution.py:263
  28.6 1.2 %collective-permute-done.6.rest_1_.far = bf16[256,896]{1,0:T(8,128)(2,1)S(1)} collective-permute-done((bf16[256,896]{1,0:T(8,128)(2,1)S(1)}, bf16[256,896]{1,0:T(8,128)(2,1)S(1)}, u32[]{:S(2)}, u32[]{:S(2)}) %collective-permute-start.6) | collective-permute-done | bytes 458784 | tf_op jit(solution)/shard_map/ppermute | solution.py:301
  30.0 3.1 %collective-permute-start.7 = (bf16[256,128]{1,0:T(8,128)(2,1)S(1)}, bf16[256,128]{1,0:T(8,128)(2,1)S(1)}, u32[]{:S(2)}, u32[]{:S(2)}) collective-permute-start(bf16[256,128]{1,0:T(8,128)(2,1)S(1)} %slice.12), channel_id=1, source_target_pairs={{0,4},{2,6},{4,0},{6,2},{8,12},{10,14},{12,8},{14,10},{16,20},{18,... | collective-permute-start | bytes 196616 | tf_op jit(solution)/shard_map/ppermute | solution.py:305
  33.1 0.1 collective-permute-start.10
  33.2 0.8 %slice_convert_fusion.rest_3_.rest_0_ = f32[1,4096]{1,0:T(1,128)S(1)} fusion(bf16[513,4096]{1,0:T(8,128)(2,1)} %taps), kind=kLoop, calls=%fused_computation.2 | loop fusion | flops 4096 | bytes 24576 | tf_op jit(solution)/shard_map/convert_element_type | solution.py:378
  34.0 1.8 %shard_map.69 = (f32[256,768]{1,0:T(8,128)S(1)}, f32[256,768]{1,0:T(8,128)S(1)}) custom-call(bf16[256,256]{1,0:T(8,128)(2,1)S(1)} %copy-done.1, bf16[256,768]{1,0:T(8,128)(2,1)S(1)} %shard_map.65.own, bf16[256,768]{1,0:T(8,128)(2,1)S(1)} %collective-permute-done.1.far, bf16[256,896]{1,0:T(8,128)(2,1)S(1)} %shard_map.66.rest_0_.own, ...), custom_call_target="tpu_custom_call" | custom-call | tf_op jit(solution)/shard_map/pallas_call | solution.py:278
  35.8 1.3 %shard_map.70 = (f32[256,768]{1,0:T(8,128)S(1)}, f32[256,768]{1,0:T(8,128)S(1)}) custom-call(bf16[256,256]{1,0:T(8,128)(2,1)S(1)} %copy-done.1, bf16[256,896]{1,0:T(8,128)(2,1)S(1)} %shard_map.66.rest_0_.own, bf16[256,896]{1,0:T(8,128)(2,1)S(1)} %collective-permute-done.6.rest_1_.far, f32[256,2048]{1,0:T(8,128)S(1)} %get-tuple-element.72.rest_2_.rest_0_.rest_9_.rest_6_, ...), custom_call_target="tpu_custom_call" | custom-call | tf_op jit(solution)/shard_map/pallas_call | solution.py:278
  37.1 1.2 %shard_map.71 = (f32[256,512]{1,0:T(8,128)S(1)}, f32[256,512]{1,0:T(8,128)S(1)}) custom-call(bf16[256,256]{1,0:T(8,128)(2,1)S(1)} %copy-done.1, bf16[256,512]{1,0:T(8,128)(2,1)S(1)} %shard_map.67.own, bf16[256,512]{1,0:T(8,128)(2,1)S(1)} %collective-permute-done.8.far, bf16[256,896]{1,0:T(8,128)(2,1)S(1)} %shard_map.66.rest_0_.own, ...), custom_call_target="tpu_custom_call" | custom-call | tf_op jit(solution)/shard_map/pallas_call | solution.py:278
  38.4 2.1 %shard_map.72 = (bf16[128,768]{1,0:T(8,128)(2,1)S(1)}, bf16[128,768]{1,0:T(8,128)(2,1)S(1)}) custom-call(s32[1]{0:T(128)} %bitcast.core, bf16[256,256]{1,0:T(8,128)(2,1)S(1)} %copy-done.1, bf16[128,768]{1,0:T(8,128)(2,1)S(1)} %copy-done.2, bf16[256,768]{1,0:T(8,128)(2,1)S(1)} %shard_map.65.own, bf16[256,768]{1,0:T(8,128)(2,1)S(1)} %collective-permute-done.1.far, ...), custom_call_target="tpu_custom_call" | custom-call | tf_op jit(solution)/shard_map/pallas_call | solution.py:290
  40.5 1.5 %shard_map.73 = (bf16[128,512]{1,0:T(8,128)(2,1)S(1)}, bf16[128,512]{1,0:T(8,128)(2,1)S(1)}) custom-call(s32[1]{0:T(128)} %bitcast.core, bf16[256,256]{1,0:T(8,128)(2,1)S(1)} %copy-done.1, bf16[128,768]{1,0:T(8,128)(2,1)S(1)} %copy-done.2, bf16[256,512]{1,0:T(8,128)(2,1)S(1)} %shard_map.67.own, bf16[256,512]{1,0:T(8,128)(2,1)S(1)} %collective-permute-done.8.far, ...), custom_call_target="tpu_custom_call" | custom-call | tf_op jit(solution)/shard_map/pallas_call | solution.py:290
  42.0 0.8 %collective-permute-done.10.near = bf16[256,768]{1,0:T(8,128)(2,1)S(1)} collective-permute-done((bf16[256,768]{1,0:T(8,128)(2,1)S(1)}, bf16[256,768]{1,0:T(8,128)(2,1)S(1)}, u32[]{:S(2)}, u32[]{:S(2)}) %collective-permute-start.10) | collective-permute-done | bytes 393248 | tf_op jit(solution)/shard_map/ppermute | solution.py:305
  42.8 1.7 %shard_map.74 = (bf16[128,768]{1,0:T(8,128)(2,1)S(1)}, bf16[128,768]{1,0:T(8,128)(2,1)S(1)}) custom-call(s32[1]{0:T(128)} %bitcast.core, bf16[256,256]{1,0:T(8,128)(2,1)S(1)} %copy-done.1, bf16[128,768]{1,0:T(8,128)(2,1)S(1)} %copy-done.2, bf16[256,896]{1,0:T(8,128)(2,1)S(1)} %shard_map.66.rest_0_.own, ...), custom_call_target="tpu_custom_call" | custom-call | tf_op jit(solution)/shard_map/pallas_call | solution.py:290
  44.5 2.6 %collective-permute-start.12 = (bf16[128,768]{1,0:T(8,128)(2,1)S(1)}, bf16[128,768]{1,0:T(8,128)(2,1)S(1)}, u32[]{:S(2)}, u32[]{:S(2)}) collective-permute-start(bf16[128,768]{1,0:T(8,128)(2,1)S(1)} %get-tuple-element.105), channel_id=1, source_target_pairs={{0,2},{2,0},{4,6},{6,4},{8,10},{10,8},{12,14},{14,12},{16,18},{18,... | collective-permute-start | bytes 589832 | tf_op jit(solution)/shard_map/ppermute | solution.py:305
  47.1 0.1 collective-permute-start.11
  47.1 0.4 collective-permute-start.13
  47.6 1.1 %collective-permute-done.13.rest_5_ = bf16[128,512]{1,0:T(8,128)(2,1)S(1)} collective-permute-done((bf16[128,512]{1,0:T(8,128)(2,1)S(1)}, bf16[128,512]{1,0:T(8,128)(2,1)S(1)}, u32[]{:S(2)}, u32[]{:S(2)}) %collective-permute-start.13) | collective-permute-done | bytes 131104 | tf_op jit(solution)/shard_map/ppermute | solution.py:305
  48.7 1.0 %shard_map.75 = bf16[128,4096]{1,0:T(8,128)(2,1)} custom-call(s32[1]{0:T(128)} %bitcast.core, bf16[128,768]{1,0:T(8,128)(2,1)S(1)} %get-tuple-element.93.rest_0_, bf16[128,768]{1,0:T(8,128)(2,1)S(1)} %get-tuple-element.102.rest_1_, bf16[128,512]{1,0:T(8,128)(2,1)S(1)} %get-tuple-element.103.rest_2_, bf16[128,768]{1,0:T(8,128)(2,1)S(1)} %collective-permute-done.11.rest_3_, ...), custom_call_target="tpu_custom_call" | custom-call | tf_op jit(solution)/shard_map/pallas_call | solution.py:424
  (22 shorter events, 0.2 us)
Async XLA Ops:
  1.5 2.3 %collective-permute-start = (bf16[128,2048]{1,0:T(8,128)(2,1)S(1)}, bf16[128,2048]{1,0:T(8,128)(2,1)S(1)}, u32[]{:S(2)}, u32[]{:S(2)}) collective-permute-start(bf16[128,2048]{1,0:T(8,128)(2,1)S(1)} %get-tuple-element.57), channel_id=1, source_target_pairs={{0,2},{2,0},{4,6},{6,4},{8,10},{10,8},{12,14},{14,12},{16,18},{18,... | collective-permute-start | bytes 1572872 | tf_op jit(solution)/shard_map/ppermute | solution.py:305
  3.9 19.1 %copy-start = (bf16[128,4096]{1,0:T(8,128)(2,1)S(1)}, bf16[128,4096]{1,0:T(8,128)(2,1)}, u32[]{:S(2)}) copy-start(bf16[128,4096]{1,0:T(8,128)(2,1)} %rest_2_) | copy-start | bytes 3145732
  3.9 21.2 %copy-start.1 = (bf16[256,256]{1,0:T(8,128)(2,1)S(1)}, bf16[256,256]{1,0:T(8,128)(2,1)}, u32[]{:S(2)}) copy-start(bf16[256,256]{1,0:T(8,128)(2,1)} %constant.39.clone.forward) | copy-start | bytes 393220
  3.9 16.2 %collective-permute-start.1 = (bf16[256,768]{1,0:T(8,128)(2,1)S(1)}, bf16[256,768]{1,0:T(8,128)(2,1)S(1)}, u32[]{:S(2)}, u32[]{:S(2)}) collective-permute-start(bf16[256,768]{1,0:T(8,128)(2,1)S(1)} %shard_map.65.own), channel_id=1, source_target_pairs={{0,8},{2,10},{4,12},{6,14},{8,16},{10,18},{12,20},{14,22},{16,24},... | collective-permute-start | bytes 1179656 | tf_op jit(solution)/shard_map/ppermute | solution.py:301
  7.3 15.5 %collective-permute-start.4 = (bf16[256,512]{1,0:T(8,128)(2,1)S(1)}, bf16[256,512]{1,0:T(8,128)(2,1)S(1)}, u32[]{:S(2)}, u32[]{:S(2)}) collective-permute-start(bf16[256,512]{1,0:T(8,128)(2,1)S(1)} %shard_map.67.own), channel_id=1, source_target_pairs={{0,4},{2,6},{4,8},{6,10},{8,12},{10,14},{12,16},{14,18},{16,20},{1... | collective-permute-start | bytes 786440 | tf_op jit(solution)/shard_map/ppermute | solution.py:301
  10.4 2.8 %collective-permute-start.2 = (f32[8,128]{1,0:T(8,128)S(1)}, f32[8,128]{1,0:T(8,128)S(1)}, u32[]{:S(2)}, u32[]{:S(2)}) collective-permute-start(f32[8,128]{1,0:T(8,128)S(1)} %get-tuple-element.58), channel_id=1, source_target_pairs={{0,1},{1,0},{2,3},{3,2},{4,5},{5,4},{6,7},{7,6},{8,9},{9,8},{10,11... | collective-permute-start | bytes 12296 | tf_op jit(solution)/shard_map/ppermute | solution.py:305
  13.2 2.6 %collective-permute-start.3 = (f32[8,128]{1,0:T(8,128)S(1)}, f32[8,128]{1,0:T(8,128)S(1)}, u32[]{:S(2)}, u32[]{:S(2)}) collective-permute-start(f32[8,128]{1,0:T(8,128)S(1)} %add.13.squares), channel_id=1, source_target_pairs={{0,2},{2,0},{4,6},{6,4},{8,10},{10,8},{12,14},{14,12},{16,18},{18,... | collective-permute-start | bytes 12296 | tf_op jit(solution)/shard_map/ppermute | solution.py:305
  16.2 13.6 %collective-permute-start.6 = (bf16[256,896]{1,0:T(8,128)(2,1)S(1)}, bf16[256,896]{1,0:T(8,128)(2,1)S(1)}, u32[]{:S(2)}, u32[]{:S(2)}) collective-permute-start(bf16[256,896]{1,0:T(8,128)(2,1)S(1)} %shard_map.66.rest_0_.own), channel_id=1, source_target_pairs={{0,8},{2,10},{4,12},{6,14},{8,16},{10,18},{12,20},{14,22},{16,24},... | collective-permute-start | bytes 1376264 | tf_op jit(solution)/shard_map/ppermute | solution.py:301
  18.2 18.9 %collective-permute-start.8 = (bf16[256,512]{1,0:T(8,128)(2,1)S(1)}, bf16[256,512]{1,0:T(8,128)(2,1)S(1)}, u32[]{:S(2)}, u32[]{:S(2)}) collective-permute-start(bf16[256,512]{1,0:T(8,128)(2,1)S(1)} %shard_map.67.own), channel_id=1, source_target_pairs={{0,8},{2,10},{4,12},{6,14},{8,16},{10,18},{12,20},{14,22},{16,24},... | collective-permute-start | bytes 786440 | tf_op jit(solution)/shard_map/ppermute | solution.py:301
  22.8 15.5 %collective-permute-start.5 = (bf16[256,768]{1,0:T(8,128)(2,1)S(1)}, bf16[256,768]{1,0:T(8,128)(2,1)S(1)}, u32[]{:S(2)}, u32[]{:S(2)}) collective-permute-start(bf16[256,768]{1,0:T(8,128)(2,1)S(1)} %broadcast_select_fusion.1), channel_id=1, source_target_pairs={{0,4},{2,6},{4,0},{6,2},{8,12},{10,14},{12,8},{14,10},{16,20},{18,... | collective-permute-start | bytes 1179656 | tf_op jit(solution)/shard_map/ppermute | solution.py:305
  22.9 15.4 %collective-permute-start.9 = (bf16[128,4096]{1,0:T(8,128)(2,1)S(1)}, bf16[128,4096]{1,0:T(8,128)(2,1)S(1)}, u32[]{:S(2)}, u32[]{:S(2)}) collective-permute-start(bf16[128,4096]{1,0:T(8,128)(2,1)S(1)} %copy-done), channel_id=1, source_target_pairs={{0,2},{2,0},{4,6},{6,4},{8,10},{10,8},{12,14},{14,12},{16,18},{18,... | collective-permute-start | bytes 3145736 | tf_op jit(solution)/shard_map/ppermute | solution.py:305
  30.0 8.4 %collective-permute-start.7 = (bf16[256,128]{1,0:T(8,128)(2,1)S(1)}, bf16[256,128]{1,0:T(8,128)(2,1)S(1)}, u32[]{:S(2)}, u32[]{:S(2)}) collective-permute-start(bf16[256,128]{1,0:T(8,128)(2,1)S(1)} %slice.12), channel_id=1, source_target_pairs={{0,4},{2,6},{4,0},{6,2},{8,12},{10,14},{12,8},{14,10},{16,20},{18,... | collective-permute-start | bytes 196616 | tf_op jit(solution)/shard_map/ppermute | solution.py:305
  33.1 9.7 %collective-permute-start.10 = (bf16[256,768]{1,0:T(8,128)(2,1)S(1)}, bf16[256,768]{1,0:T(8,128)(2,1)S(1)}, u32[]{:S(2)}, u32[]{:S(2)}) collective-permute-start(bf16[256,768]{1,0:T(8,128)(2,1)S(1)} %slice.13), channel_id=1, source_target_pairs={{0,4},{2,6},{4,0},{6,2},{8,12},{10,14},{12,8},{14,10},{16,20},{18,... | collective-permute-start | bytes 1179656 | tf_op jit(solution)/shard_map/ppermute | solution.py:305
  37.1 1.3 %copy-start.2 = (bf16[128,768]{1,0:T(8,128)(2,1)S(1)}, bf16[128,768]{1,0:T(8,128)(2,1)}, u32[]{:S(2)}) copy-start(bf16[128,768]{1,0:T(8,128)(2,1)} %constant.40.clone.back) | copy-start | bytes 589828
  37.1 1.3 %copy-start.3 = (f32[4096]{0:T(1024)S(1)}, f32[4096]{0:T(1024)}, u32[]{:S(2)}) copy-start(f32[4096]{0:T(1024)} %param.9) | copy-start | bytes 49156
  44.5 4.2 %collective-permute-start.12 = (bf16[128,768]{1,0:T(8,128)(2,1)S(1)}, bf16[128,768]{1,0:T(8,128)(2,1)S(1)}, u32[]{:S(2)}, u32[]{:S(2)}) collective-permute-start(bf16[128,768]{1,0:T(8,128)(2,1)S(1)} %get-tuple-element.105), channel_id=1, source_target_pairs={{0,2},{2,0},{4,6},{6,4},{8,10},{10,8},{12,14},{14,12},{16,18},{18,... | collective-permute-start | bytes 589832 | tf_op jit(solution)/shard_map/ppermute | solution.py:305
  47.1 1.6 %collective-permute-start.11 = (bf16[128,768]{1,0:T(8,128)(2,1)S(1)}, bf16[128,768]{1,0:T(8,128)(2,1)S(1)}, u32[]{:S(2)}, u32[]{:S(2)}) collective-permute-start(bf16[128,768]{1,0:T(8,128)(2,1)S(1)} %get-tuple-element.104), channel_id=1, source_target_pairs={{0,2},{2,0},{4,6},{6,4},{8,10},{10,8},{12,14},{14,12},{16,18},{18,... | collective-permute-start | bytes 589832 | tf_op jit(solution)/shard_map/ppermute | solution.py:305
  47.1 1.6 %collective-permute-start.13 = (bf16[128,512]{1,0:T(8,128)(2,1)S(1)}, bf16[128,512]{1,0:T(8,128)(2,1)S(1)}, u32[]{:S(2)}, u32[]{:S(2)}) collective-permute-start(bf16[128,512]{1,0:T(8,128)(2,1)S(1)} %get-tuple-element.106), channel_id=1, source_target_pairs={{0,2},{2,0},{4,6},{6,4},{8,10},{10,8},{12,14},{14,12},{16,18},{18,... | collective-permute-start | bytes 393224 | tf_op jit(solution)/shard_map/ppermute | solution.py:305

commit v3 on v2

--- a/solution.py
+++ b/solution.py
@@ -12,10 +12,11 @@
 BF16 = jnp.bfloat16
 F32 = jnp.float32
 EPS = 1e-06
-CFG = dict(tile=256, cuts=(6, 6), g=1, hk=1, t=0, w=0, p=0, s=1, f=1)
+CFG = dict(tile=256, cuts=(6, 6), g=1, hk=1, t=0, w=0, p=0, s=1, f=1, l=0)
 GROUP = 4
 LANES = 128
 PARTS = 3
+RIDER = 16
 PARAMS = pltpu.CompilerParams(vmem_limit_bytes=24 * 2**20)
 SMEM = pl.BlockSpec(memory_space=pltpu.SMEM)
 VMEM = pl.BlockSpec(memory_space=pltpu.VMEM)
@@ -115,27 +116,26 @@
 
 
 def pack_body(total_channels, start, core, mine, given, squares, given_squares, out):
-    rows = mine.shape[0]
-    lane = lax.broadcasted_iota(jnp.int32, (rows, LANES), 1)
-    columns = [column_of(squares), column_of(given_squares)]
-    factors = [lax.rsqrt(column / total_channels + EPS) for column in columns]
-    tails = []
-    for left in columns:
-        tail = jnp.zeros((rows, LANES), F32)
-        for k in range(PARTS):
-            piece = left.astype(BF16).astype(F32)
-            left = left - piece
-            tail = jnp.where(lane == k, piece, tail)
-        tails.append(tail.astype(BF16))
-    width = out.shape[1] - LANES
+    rows, width = mine.shape[0], out.shape[1]
+    sums = (squares, given_squares)
+    factors = [lax.rsqrt(column_of(s) / total_channels + EPS) for s in sums]
+    line = lax.broadcasted_iota(jnp.int32, (RIDER, rows), 0)
     for which in range(2):
 
         @pl.when(core[0] == which)
         def _():
-            for block, factor, tail, place in zip((mine, given), factors, tails, (which, 1 - which)):
-                there = slice(place * rows, (place + 1) * rows)
-                out[there, :width] = (block[:, start : start + width].astype(F32) * factor).astype(BF16)
-                out[there, width:] = tail
+            tail = jnp.zeros((RIDER, rows), F32)
+            for block, factor, left, place in zip((mine, given), factors, sums, (which, 1 - which)):
+                part = block[:, start : start + width].astype(F32) * factor
+                out[place * rows : (place + 1) * rows, :] = part.astype(BF16)
+                left = left[0:1, :]
+                for k in range(PARTS):
+                    piece = left.astype(BF16).astype(F32)
+                    left = left - piece
+                    tail = jnp.where(line == place * RIDER // 2 + k, piece, tail)
+            out[2 * rows :, :rows] = tail.astype(BF16)
+            if width > rows:
+                out[2 * rows :, rows:] = jnp.zeros((RIDER, width - rows), BF16)
 
 
 def spectra_body(tile, core, forward, taps, *rest):
@@ -175,26 +175,29 @@
     return sum0, plus(sums[1], times(far1, h4))
 
 
-def blocks(total_channels, block, part, packed):
-    rows = block.shape[0] // 2
+def blocks(total_channels, rows, block, part, packed):
     halves = [block[j * rows : (j + 1) * rows, part] for j in range(2)]
     if packed is None:
         return halves
-    begin = packed.shape[1] - LANES
-    sums = sum(packed[:, begin + k : begin + k + 1].astype(F32) for k in range(PARTS))
-    factor = lax.rsqrt(sums / total_channels + EPS)
-    return [(half.astype(F32) * factor[j * rows : (j + 1) * rows]).astype(BF16) for j, half in enumerate(halves)]
+    parts = packed[packed.shape[0] - RIDER :, :rows].astype(F32)
+    outs = []
+    for j, half in enumerate(halves):
+        sums = sum(parts[j * RIDER // 2 + k : j * RIDER // 2 + k + 1, :] for k in range(PARTS))
+        factor = lax.rsqrt(column_of(sums) / total_channels + EPS)
+        outs.append((half.astype(F32) * factor).astype(BF16))
+    return outs
 
 
 def first_body(total_channels, tile, start, raw, forward, own, far, *rest):
     packed = rest[:2] if raw else (None, None)
     *h, sum0_out, sum1_out = rest[2:] if raw else rest
     table = forward[...]
+    rows = table.shape[0] // 2
     for k in range(sum0_out.shape[1] // tile):
         part = slice(k * tile, (k + 1) * tile)
         wide = slice(start + k * tile, start + (k + 1) * tile)
-        own0, own1 = (spectrum(table, b) for b in blocks(total_channels, own, part, packed[0]))
-        far0, far1 = (spectrum(table, b) for b in blocks(total_channels, far, part, packed[1]))
+        own0, own1 = (spectrum(table, b) for b in blocks(total_channels, rows, own, part, packed[0]))
+        far0, far1 = (spectrum(table, b) for b in blocks(total_channels, rows, far, part, packed[1]))
         same, next_ = load(h[0], wide), load(h[1], wide)
         sums = times(own0, same), plus(times(own1, same), times(own0, next_))
         sums = far_terms(far0, far1, sums, h, wide)
@@ -207,6 +210,7 @@
     last, skip, gate, given_gate, sum0, sum1, *h, own_out, given_out = rest[3:] if raw else rest
     half = gate.shape[1] // 2
     table = forward[...]
+    rows = table.shape[0] // 2
     inverse = back[...]
     first = core[0] * half + start
 
@@ -220,9 +224,9 @@
         part = slice(k * tile, (k + 1) * tile)
         local = slice(start + k * tile, start + (k + 1) * tile)
         wide = pl.ds(pl.multiple_of(first + k * tile, LANES), tile)
-        near0, near1 = (spectrum(table, b) for b in blocks(total_channels, near, part, packed[2]))
+        near0, near1 = (spectrum(table, b) for b in blocks(total_channels, rows, near, part, packed[2]))
         sums = near_terms(near0, near1, (load(sum0, part), load(sum1, part)), h, local)
-        here, there = blocks(total_channels, own, part, packed[0]), blocks(total_channels, far, part, packed[1])
+        here, there = blocks(total_channels, rows, own, part, packed[0]), blocks(total_channels, rows, far, part, packed[1])
         values = []
         for j in range(2):
             value = restored(sums[j]) + last[:, wide] * there[j].astype(F32)
@@ -279,13 +283,13 @@
         functools.partial(first_body, total_channels, tile_of(width), start, bool(packed)),
         in_specs=[VMEM] * len(operands),
         out_specs=[VMEM] * 2,
-        out_shape=[jax.ShapeDtypeStruct((blocks[0].shape[0], width), F32)] * 2,
+        out_shape=[jax.ShapeDtypeStruct((forward.shape[0], width), F32)] * 2,
         compiler_params=PARAMS,
     )(*operands)
 
 
 def second_part(total_channels, core, forward, back, blocks, packed, small, gates, sums, h, start, width):
-    shape = jax.ShapeDtypeStruct((blocks[0].shape[0] // 2, width), BF16)
+    shape = jax.ShapeDtypeStruct((forward.shape[0] // 2, width), BF16)
     operands = [core, forward, back, *blocks, *packed, *small, *gates, *sums, *h]
     return pl.pallas_call(
         functools.partial(second_body, total_channels, tile_of(width), start, bool(packed)),
@@ -368,7 +372,7 @@
         functools.partial(pack_body, total_channels, starts[1]),
         in_specs=[SMEM] + [VMEM] * 4,
         out_specs=VMEM,
-        out_shape=jax.ShapeDtypeStruct((2 * rows, cuts[1] + LANES), BF16),
+        out_shape=jax.ShapeDtypeStruct((2 * rows + RIDER, cuts[1]), BF16),
         compiler_params=PARAMS,
     )(core_arg, mine, given, squares, given_squares)
     if CFG["w"]:
@@ -385,6 +389,8 @@
     far[0], own[1] = tie((far[0], own[1]))
     if CFG["s"]:
         far[0], straight = tie((far[0], straight))
+    if CFG["l"]:
+        far[0], last = tie((far[0], last))
     near = [turned(0), None, straight]
     if CFG["hk"] == 1:
         taps, far[0] = tie((taps, far[0]))
@@ -392,8 +398,8 @@
     if CFG["hk"] == 1:
         far[1], h = tie((far[1], h))
     sent = jnp.where(on_low, own[1], far[1])
-    near_rider = swapped_with(sent[:, cuts[1] :], "seq", 2)
-    near[1] = swapped_with(sent[:, : cuts[1]], "seq", 2)
+    near_rider = swapped_with(sent[2 * rows :], "seq", 2)
+    near[1] = swapped_with(sent[: 2 * rows], "seq", 2)
     if CFG["g"] == 1:
         gating, far[0] = tie((gating, far[0]))
     if CFG["g"] == 2:

time: 50.1 us -> 48.9 us (0.976)
  waiting for transfers between devices: 9.76 us -> 8.19 us
    ppermute x4, waiting for transfers between devices: 3.95 us -> 3.07 us  [shifted(): lax.ppermute(value, 'seq', [(s, s + steps) for s in range(count - steps)])]
    ppermute x10, waiting for transfers between devices: 5.81 us -> 5.11 us  [swapped_with(): lax.ppermute(value, axis, [(s, s ^ bit) for s in range(lax.axis_size(axis...]
    ppermute x10, starting transfers between devices: 12.3 us -> 12.8 us  [swapped_with(): lax.ppermute(value, axis, [(s, s ^ bit) for s in range(lax.axis_size(axis...]
where the time goes in v3:
time: 48.9 us; the launch traced here: 48.4 us
  starting transfers between devices  23.1 us (47%)
  Pallas kernels  15.8 us (32%)
  waiting for transfers between devices  8.19 us (17%)
  other arithmetic  0.95 us (2%)
    ppermute x10, starting transfers between devices, swapped_with(): lax.ppermute(value, axis, [(s, s ^ bit) for s in range(lax.axis_size(axis...  12.8 us
    ppermute x4, starting transfers between devices, shifted(): lax.ppermute(value, 'seq', [(s, s + steps) for s in range(count - steps)])  10.3 us
    pallas_call x3, Pallas kernels, second_part(): pl.pallas_call(functools.partial(second_body, total_channels, tile_of(wid...  5.24 us
    ppermute x10, waiting for transfers between devices, swapped_with(): lax.ppermute(value, axis, [(s, s ^ bit) for s in range(lax.axis_size(axis...  5.11 us
    pallas_call x3, Pallas kernels, first_part(): pl.pallas_call(functools.partial(first_body, total_channels, tile_of(widt...  4.14 us
    pallas_call x1, Pallas kernels, spectra(): pl.pallas_call(functools.partial(spectra_body, tile), in_specs=[SMEM, VME...  3.56 us
    ppermute x4, waiting for transfers between devices, shifted(): lax.ppermute(value, 'seq', [(s, s + steps) for s in range(count - steps)])  3.07 us
    pallas_call x1, Pallas kernels, on_device(): pl.pallas_call(front_body, in_specs=[SMEM, HBM], out_specs=[VMEM] * 3, ou...  1.54 us
  transfers between devices with their start and end apart: 14, of which 7 were waited for; matrix products, arithmetic and copies ran while one was open for 2% of the time, Pallas kernels for 24%

profile of v3, /device:TPU:17, one launch (start us, length us, event | category | flops | bytes accessed | tf_op | source)
XLA Modules:
  0.0 48.4 jit_solution(9537657084317906304)
XLA Ops:
  0.0 1.5 %shard_map.64 = (f32[8,128]{1,0:T(8,128)S(1)}, bf16[128,2048]{1,0:T(8,128)(2,1)S(1)}, bf16[128,2048]{1,0:T(8,128)(2,1)S(1)}) custom-call(s32[1]{0:T(128)} %bitcast.core, bf16[128,4096]{1,0:T(8,128)(2,1)} %x.1), custom_call_target="tpu_custom_call" | custom-call | tf_op jit(solution)/shard_map/pallas_call | solution.py:340
  1.5 0.7 %collective-permute-start = (bf16[128,2048]{1,0:T(8,128)(2,1)S(1)}, bf16[128,2048]{1,0:T(8,128)(2,1)S(1)}, u32[]{:S(2)}, u32[]{:S(2)}) collective-permute-start(bf16[128,2048]{1,0:T(8,128)(2,1)S(1)} %get-tuple-element.57), channel_id=1, source_target_pairs={{0,2},{2,0},{4,6},{6,4},{8,10},{10,8},{12,14},{14,12},{16,18},{18,... | collective-permute-start | bytes 1572872 | tf_op jit(solution)/shard_map/ppermute | solution.py:309
  2.3 1.5 %collective-permute-done.given = bf16[128,2048]{1,0:T(8,128)(2,1)S(1)} collective-permute-done((bf16[128,2048]{1,0:T(8,128)(2,1)S(1)}, bf16[128,2048]{1,0:T(8,128)(2,1)S(1)}, u32[]{:S(2)}, u32[]{:S(2)}) %collective-permute-start) | collective-permute-done | bytes 524320 | tf_op jit(solution)/shard_map/ppermute | solution.py:309
  3.9 3.3 %collective-permute-start.1 = (bf16[256,768]{1,0:T(8,128)(2,1)S(1)}, bf16[256,768]{1,0:T(8,128)(2,1)S(1)}, u32[]{:S(2)}, u32[]{:S(2)}) collective-permute-start(bf16[256,768]{1,0:T(8,128)(2,1)S(1)} %shard_map.65.own), channel_id=1, source_target_pairs={{0,8},{2,10},{4,12},{6,14},{8,16},{10,18},{12,20},{14,22},{16,24},... | collective-permute-start | bytes 1179656 | tf_op jit(solution)/shard_map/ppermute | solution.py:305
  7.3 3.1 %collective-permute-start.4 = (bf16[256,512]{1,0:T(8,128)(2,1)S(1)}, bf16[256,512]{1,0:T(8,128)(2,1)S(1)}, u32[]{:S(2)}, u32[]{:S(2)}) collective-permute-start(bf16[256,512]{1,0:T(8,128)(2,1)S(1)} %shard_map.67.own), channel_id=1, source_target_pairs={{0,4},{2,6},{4,8},{6,10},{8,12},{10,14},{12,16},{14,18},{16,20},{1... | collective-permute-start | bytes 786440 | tf_op jit(solution)/shard_map/ppermute | solution.py:305
  10.4 1.3 %collective-permute-start.2 = (f32[8,128]{1,0:T(8,128)S(1)}, f32[8,128]{1,0:T(8,128)S(1)}, u32[]{:S(2)}, u32[]{:S(2)}) collective-permute-start(f32[8,128]{1,0:T(8,128)S(1)} %get-tuple-element.58), channel_id=1, source_target_pairs={{0,1},{1,0},{2,3},{3,2},{4,5},{5,4},{6,7},{7,6},{8,9},{9,8},{10,11... | collective-permute-start | bytes 12296 | tf_op jit(solution)/shard_map/ppermute | solution.py:309
  11.7 1.5 %collective-permute-done.2 = f32[8,128]{1,0:T(8,128)S(1)} collective-permute-done((f32[8,128]{1,0:T(8,128)S(1)}, f32[8,128]{1,0:T(8,128)S(1)}, u32[]{:S(2)}, u32[]{:S(2)}) %collective-permute-start.2) | collective-permute-done | bytes 4128 | tf_op jit(solution)/shard_map/ppermute | solution.py:309
  13.2 1.8 %collective-permute-start.3 = (f32[8,128]{1,0:T(8,128)S(1)}, f32[8,128]{1,0:T(8,128)S(1)}, u32[]{:S(2)}, u32[]{:S(2)}) collective-permute-start(f32[8,128]{1,0:T(8,128)S(1)} %add.13.squares), channel_id=1, source_target_pairs={{0,2},{2,0},{4,6},{6,4},{8,10},{10,8},{12,14},{14,12},{16,18},{18,... | collective-permute-start | bytes 12296 | tf_op jit(solution)/shard_map/ppermute | solution.py:309
  15.0 0.8 %collective-permute-done.3.given_squares = f32[8,128]{1,0:T(8,128)S(1)} collective-permute-done((f32[8,128]{1,0:T(8,128)S(1)}, f32[8,128]{1,0:T(8,128)S(1)}, u32[]{:S(2)}, u32[]{:S(2)}) %collective-permute-start.3) | collective-permute-done | bytes 4128 | tf_op jit(solution)/shard_map/ppermute | solution.py:309
  15.9 0.2 shard_map.66.rest_0_.own
  16.1 1.9 %collective-permute-start.6 = (bf16[272,768]{1,0:T(8,128)(2,1)S(1)}, bf16[272,768]{1,0:T(8,128)(2,1)S(1)}, u32[]{:S(2)}, u32[]{:S(2)}) collective-permute-start(bf16[272,768]{1,0:T(8,128)(2,1)S(1)} %shard_map.66.rest_0_.own), channel_id=1, source_target_pairs={{0,8},{2,10},{4,12},{6,14},{8,16},{10,18},{12,20},{14,22},{16,24},... | collective-permute-start | bytes 1253384 | tf_op jit(solution)/shard_map/ppermute | solution.py:305
  18.1 1.9 %collective-permute-start.8 = (bf16[256,512]{1,0:T(8,128)(2,1)S(1)}, bf16[256,512]{1,0:T(8,128)(2,1)S(1)}, u32[]{:S(2)}, u32[]{:S(2)}) collective-permute-start(bf16[256,512]{1,0:T(8,128)(2,1)S(1)} %shard_map.67.own), channel_id=1, source_target_pairs={{0,8},{2,10},{4,12},{6,14},{8,16},{10,18},{12,20},{14,22},{16,24},... | collective-permute-start | bytes 786440 | tf_op jit(solution)/shard_map/ppermute | solution.py:305
  20.0 2.8 %collective-permute-done.4.near = bf16[256,512]{1,0:T(8,128)(2,1)S(1)} collective-permute-done((bf16[256,512]{1,0:T(8,128)(2,1)S(1)}, bf16[256,512]{1,0:T(8,128)(2,1)S(1)}, u32[]{:S(2)}, u32[]{:S(2)}) %collective-permute-start.4) | collective-permute-done | bytes 262176 | tf_op jit(solution)/shard_map/ppermute | solution.py:305
  22.8 0.1 collective-permute-start.5
  22.9 2.1 %collective-permute-start.9 = (bf16[128,4096]{1,0:T(8,128)(2,1)S(1)}, bf16[128,4096]{1,0:T(8,128)(2,1)S(1)}, u32[]{:S(2)}, u32[]{:S(2)}) collective-permute-start(bf16[128,4096]{1,0:T(8,128)(2,1)S(1)} %copy-done), channel_id=1, source_target_pairs={{0,2},{2,0},{4,6},{6,4},{8,10},{10,8},{12,14},{14,12},{16,18},{18,... | collective-permute-start | bytes 3145736 | tf_op jit(solution)/shard_map/ppermute | solution.py:309
  25.0 3.6 %shard_map.68 = (f32[256,2048]{1,0:T(8,128)S(1)}, f32[256,2048]{1,0:T(8,128)S(1)}, f32[256,2048]{1,0:T(8,128)S(1)}, f32[256,2048]{1,0:T(8,128)S(1)}, f32[256,2048]{1,0:T(8,128)S(1)}) custom-call(s32[1]{0:T(128)} %bitcast.core, bf16[256,256]{1,0:T(8,128)(2,1)S(1)} %copy-done.1, bf16[513,4096]{1,0:T(8,128)(2,1)} %taps), custom_call_target="tpu_custom_call" | custom-call | tf_op jit(solution)/shard_map/pallas_call | solution.py:267
  28.6 0.3 collective-permute-done.6.rest_1_.far
  29.0 3.2 %collective-permute-start.7 = (bf16[16,768]{1,0:T(8,128)(2,1)S(1)}, bf16[16,768]{1,0:T(8,128)(2,1)S(1)}, u32[]{:S(2)}, u32[]{:S(2)}) collective-permute-start(bf16[16,768]{1,0:T(8,128)(2,1)S(1)} %slice.12), channel_id=1, source_target_pairs={{0,4},{2,6},{4,0},{6,2},{8,12},{10,14},{12,8},{14,10},{16,20},{18,... | collective-permute-start | bytes 73736 | tf_op jit(solution)/shard_map/ppermute | solution.py:309
  32.2 0.1 collective-permute-start.10
  32.3 0.8 %slice_convert_fusion.rest_3_.rest_0_ = f32[1,4096]{1,0:T(1,128)S(1)} fusion(bf16[513,4096]{1,0:T(8,128)(2,1)} %taps), kind=kLoop, calls=%fused_computation.2 | loop fusion | flops 4096 | bytes 24576 | tf_op jit(solution)/shard_map/convert_element_type | solution.py:382
  33.1 1.7 %shard_map.69 = (f32[256,768]{1,0:T(8,128)S(1)}, f32[256,768]{1,0:T(8,128)S(1)}) custom-call(bf16[256,256]{1,0:T(8,128)(2,1)S(1)} %copy-done.1, bf16[256,768]{1,0:T(8,128)(2,1)S(1)} %shard_map.65.own, bf16[256,768]{1,0:T(8,128)(2,1)S(1)} %collective-permute-done.1.far, bf16[272,768]{1,0:T(8,128)(2,1)S(1)} %shard_map.66.rest_0_.own, ...), custom_call_target="tpu_custom_call" | custom-call | tf_op jit(solution)/shard_map/pallas_call | solution.py:282
  34.9 1.3 %shard_map.70 = (f32[256,768]{1,0:T(8,128)S(1)}, f32[256,768]{1,0:T(8,128)S(1)}) custom-call(bf16[256,256]{1,0:T(8,128)(2,1)S(1)} %copy-done.1, bf16[272,768]{1,0:T(8,128)(2,1)S(1)} %shard_map.66.rest_0_.own, bf16[272,768]{1,0:T(8,128)(2,1)S(1)} %collective-permute-done.6.rest_1_.far, f32[256,2048]{1,0:T(8,128)S(1)} %get-tuple-element.72.rest_2_.rest_0_.rest_9_.rest_6_, ...), custom_call_target="tpu_custom_call" | custom-call | tf_op jit(solution)/shard_map/pallas_call | solution.py:282
  36.2 1.1 %shard_map.71 = (f32[256,512]{1,0:T(8,128)S(1)}, f32[256,512]{1,0:T(8,128)S(1)}) custom-call(bf16[256,256]{1,0:T(8,128)(2,1)S(1)} %copy-done.1, bf16[256,512]{1,0:T(8,128)(2,1)S(1)} %shard_map.67.own, bf16[256,512]{1,0:T(8,128)(2,1)S(1)} %collective-permute-done.8.far, bf16[272,768]{1,0:T(8,128)(2,1)S(1)} %shard_map.66.rest_0_.own, ...), custom_call_target="tpu_custom_call" | custom-call | tf_op jit(solution)/shard_map/pallas_call | solution.py:282
  37.4 2.0 %shard_map.72 = (bf16[128,768]{1,0:T(8,128)(2,1)S(1)}, bf16[128,768]{1,0:T(8,128)(2,1)S(1)}) custom-call(s32[1]{0:T(128)} %bitcast.core, bf16[256,256]{1,0:T(8,128)(2,1)S(1)} %copy-done.1, bf16[128,768]{1,0:T(8,128)(2,1)S(1)} %copy-done.2, bf16[256,768]{1,0:T(8,128)(2,1)S(1)} %shard_map.65.own, bf16[256,768]{1,0:T(8,128)(2,1)S(1)} %collective-permute-done.1.far, ...), custom_call_target="tpu_custom_call" | custom-call | tf_op jit(solution)/shard_map/pallas_call | solution.py:294
  39.4 1.5 %shard_map.73 = (bf16[128,512]{1,0:T(8,128)(2,1)S(1)}, bf16[128,512]{1,0:T(8,128)(2,1)S(1)}) custom-call(s32[1]{0:T(128)} %bitcast.core, bf16[256,256]{1,0:T(8,128)(2,1)S(1)} %copy-done.1, bf16[128,768]{1,0:T(8,128)(2,1)S(1)} %copy-done.2, bf16[256,512]{1,0:T(8,128)(2,1)S(1)} %shard_map.67.own, bf16[256,512]{1,0:T(8,128)(2,1)S(1)} %collective-permute-done.8.far, ...), custom_call_target="tpu_custom_call" | custom-call | tf_op jit(solution)/shard_map/pallas_call | solution.py:294
  40.9 0.1 collective-permute-done.10.near
  41.0 1.7 %shard_map.74 = (bf16[128,768]{1,0:T(8,128)(2,1)S(1)}, bf16[128,768]{1,0:T(8,128)(2,1)S(1)}) custom-call(s32[1]{0:T(128)} %bitcast.core, bf16[256,256]{1,0:T(8,128)(2,1)S(1)} %copy-done.1, bf16[128,768]{1,0:T(8,128)(2,1)S(1)} %copy-done.2, bf16[272,768]{1,0:T(8,128)(2,1)S(1)} %shard_map.66.rest_0_.own, ...), custom_call_target="tpu_custom_call" | custom-call | tf_op jit(solution)/shard_map/pallas_call | solution.py:294
  42.7 3.0 %collective-permute-start.12 = (bf16[128,768]{1,0:T(8,128)(2,1)S(1)}, bf16[128,768]{1,0:T(8,128)(2,1)S(1)}, u32[]{:S(2)}, u32[]{:S(2)}) collective-permute-start(bf16[128,768]{1,0:T(8,128)(2,1)S(1)} %get-tuple-element.105), channel_id=1, source_target_pairs={{0,2},{2,0},{4,6},{6,4},{8,10},{10,8},{12,14},{14,12},{16,18},{18,... | collective-permute-start | bytes 589832 | tf_op jit(solution)/shard_map/ppermute | solution.py:309
  45.8 0.1 collective-permute-start.11
  45.8 0.4 collective-permute-start.13
  46.3 1.1 %collective-permute-done.13.rest_5_ = bf16[128,512]{1,0:T(8,128)(2,1)S(1)} collective-permute-done((bf16[128,512]{1,0:T(8,128)(2,1)S(1)}, bf16[128,512]{1,0:T(8,128)(2,1)S(1)}, u32[]{:S(2)}, u32[]{:S(2)}) %collective-permute-start.13) | collective-permute-done | bytes 131104 | tf_op jit(solution)/shard_map/ppermute | solution.py:309
  47.4 1.0 %shard_map.75 = bf16[128,4096]{1,0:T(8,128)(2,1)} custom-call(s32[1]{0:T(128)} %bitcast.core, bf16[128,768]{1,0:T(8,128)(2,1)S(1)} %get-tuple-element.93.rest_0_, bf16[128,768]{1,0:T(8,128)(2,1)S(1)} %get-tuple-element.102.rest_1_, bf16[128,512]{1,0:T(8,128)(2,1)S(1)} %get-tuple-element.103.rest_2_, bf16[128,768]{1,0:T(8,128)(2,1)S(1)} %collective-permute-done.11.rest_3_, ...), custom_call_target="tpu_custom_call" | custom-call | tf_op jit(solution)/shard_map/pallas_call | solution.py:430
  (22 shorter events, 0.2 us)
Async XLA Ops:
  1.5 2.3 %collective-permute-start = (bf16[128,2048]{1,0:T(8,128)(2,1)S(1)}, bf16[128,2048]{1,0:T(8,128)(2,1)S(1)}, u32[]{:S(2)}, u32[]{:S(2)}) collective-permute-start(bf16[128,2048]{1,0:T(8,128)(2,1)S(1)} %get-tuple-element.57), channel_id=1, source_target_pairs={{0,2},{2,0},{4,6},{6,4},{8,10},{10,8},{12,14},{14,12},{16,18},{18,... | collective-permute-start | bytes 1572872 | tf_op jit(solution)/shard_map/ppermute | solution.py:309
  3.9 19.1 %copy-start = (bf16[128,4096]{1,0:T(8,128)(2,1)S(1)}, bf16[128,4096]{1,0:T(8,128)(2,1)}, u32[]{:S(2)}) copy-start(bf16[128,4096]{1,0:T(8,128)(2,1)} %rest_2_) | copy-start | bytes 3145732
  3.9 21.2 %copy-start.1 = (bf16[256,256]{1,0:T(8,128)(2,1)S(1)}, bf16[256,256]{1,0:T(8,128)(2,1)}, u32[]{:S(2)}) copy-start(bf16[256,256]{1,0:T(8,128)(2,1)} %constant.39.clone.forward) | copy-start | bytes 393220
  3.9 16.1 %collective-permute-start.1 = (bf16[256,768]{1,0:T(8,128)(2,1)S(1)}, bf16[256,768]{1,0:T(8,128)(2,1)S(1)}, u32[]{:S(2)}, u32[]{:S(2)}) collective-permute-start(bf16[256,768]{1,0:T(8,128)(2,1)S(1)} %shard_map.65.own), channel_id=1, source_target_pairs={{0,8},{2,10},{4,12},{6,14},{8,16},{10,18},{12,20},{14,22},{16,24},... | collective-permute-start | bytes 1179656 | tf_op jit(solution)/shard_map/ppermute | solution.py:305
  7.3 15.5 %collective-permute-start.4 = (bf16[256,512]{1,0:T(8,128)(2,1)S(1)}, bf16[256,512]{1,0:T(8,128)(2,1)S(1)}, u32[]{:S(2)}, u32[]{:S(2)}) collective-permute-start(bf16[256,512]{1,0:T(8,128)(2,1)S(1)} %shard_map.67.own), channel_id=1, source_target_pairs={{0,4},{2,6},{4,8},{6,10},{8,12},{10,14},{12,16},{14,18},{16,20},{1... | collective-permute-start | bytes 786440 | tf_op jit(solution)/shard_map/ppermute | solution.py:305
  10.4 2.8 %collective-permute-start.2 = (f32[8,128]{1,0:T(8,128)S(1)}, f32[8,128]{1,0:T(8,128)S(1)}, u32[]{:S(2)}, u32[]{:S(2)}) collective-permute-start(f32[8,128]{1,0:T(8,128)S(1)} %get-tuple-element.58), channel_id=1, source_target_pairs={{0,1},{1,0},{2,3},{3,2},{4,5},{5,4},{6,7},{7,6},{8,9},{9,8},{10,11... | collective-permute-start | bytes 12296 | tf_op jit(solution)/shard_map/ppermute | solution.py:309
  13.2 2.6 %collective-permute-start.3 = (f32[8,128]{1,0:T(8,128)S(1)}, f32[8,128]{1,0:T(8,128)S(1)}, u32[]{:S(2)}, u32[]{:S(2)}) collective-permute-start(f32[8,128]{1,0:T(8,128)S(1)} %add.13.squares), channel_id=1, source_target_pairs={{0,2},{2,0},{4,6},{6,4},{8,10},{10,8},{12,14},{14,12},{16,18},{18,... | collective-permute-start | bytes 12296 | tf_op jit(solution)/shard_map/ppermute | solution.py:309
  16.1 12.8 %collective-permute-start.6 = (bf16[272,768]{1,0:T(8,128)(2,1)S(1)}, bf16[272,768]{1,0:T(8,128)(2,1)S(1)}, u32[]{:S(2)}, u32[]{:S(2)}) collective-permute-start(bf16[272,768]{1,0:T(8,128)(2,1)S(1)} %shard_map.66.rest_0_.own), channel_id=1, source_target_pairs={{0,8},{2,10},{4,12},{6,14},{8,16},{10,18},{12,20},{14,22},{16,24},... | collective-permute-start | bytes 1253384 | tf_op jit(solution)/shard_map/ppermute | solution.py:305
  18.1 18.1 %collective-permute-start.8 = (bf16[256,512]{1,0:T(8,128)(2,1)S(1)}, bf16[256,512]{1,0:T(8,128)(2,1)S(1)}, u32[]{:S(2)}, u32[]{:S(2)}) collective-permute-start(bf16[256,512]{1,0:T(8,128)(2,1)S(1)} %shard_map.67.own), channel_id=1, source_target_pairs={{0,8},{2,10},{4,12},{6,14},{8,16},{10,18},{12,20},{14,22},{16,24},... | collective-permute-start | bytes 786440 | tf_op jit(solution)/shard_map/ppermute | solution.py:305
  22.8 14.5 %collective-permute-start.5 = (bf16[256,768]{1,0:T(8,128)(2,1)S(1)}, bf16[256,768]{1,0:T(8,128)(2,1)S(1)}, u32[]{:S(2)}, u32[]{:S(2)}) collective-permute-start(bf16[256,768]{1,0:T(8,128)(2,1)S(1)} %broadcast_select_fusion.1), channel_id=1, source_target_pairs={{0,4},{2,6},{4,0},{6,2},{8,12},{10,14},{12,8},{14,10},{16,20},{18,... | collective-permute-start | bytes 1179656 | tf_op jit(solution)/shard_map/ppermute | solution.py:309
  22.9 14.4 %collective-permute-start.9 = (bf16[128,4096]{1,0:T(8,128)(2,1)S(1)}, bf16[128,4096]{1,0:T(8,128)(2,1)S(1)}, u32[]{:S(2)}, u32[]{:S(2)}) collective-permute-start(bf16[128,4096]{1,0:T(8,128)(2,1)S(1)} %copy-done), channel_id=1, source_target_pairs={{0,2},{2,0},{4,6},{6,4},{8,10},{10,8},{12,14},{14,12},{16,18},{18,... | collective-permute-start | bytes 3145736 | tf_op jit(solution)/shard_map/ppermute | solution.py:309
  29.0 8.3 %collective-permute-start.7 = (bf16[16,768]{1,0:T(8,128)(2,1)S(1)}, bf16[16,768]{1,0:T(8,128)(2,1)S(1)}, u32[]{:S(2)}, u32[]{:S(2)}) collective-permute-start(bf16[16,768]{1,0:T(8,128)(2,1)S(1)} %slice.12), channel_id=1, source_target_pairs={{0,4},{2,6},{4,0},{6,2},{8,12},{10,14},{12,8},{14,10},{16,20},{18,... | collective-permute-start | bytes 73736 | tf_op jit(solution)/shard_map/ppermute | solution.py:309
  32.2 8.8 %collective-permute-start.10 = (bf16[256,768]{1,0:T(8,128)(2,1)S(1)}, bf16[256,768]{1,0:T(8,128)(2,1)S(1)}, u32[]{:S(2)}, u32[]{:S(2)}) collective-permute-start(bf16[256,768]{1,0:T(8,128)(2,1)S(1)} %slice.13), channel_id=1, source_target_pairs={{0,4},{2,6},{4,0},{6,2},{8,12},{10,14},{12,8},{14,10},{16,20},{18,... | collective-permute-start | bytes 1179656 | tf_op jit(solution)/shard_map/ppermute | solution.py:309
  36.2 1.2 %copy-start.2 = (bf16[128,768]{1,0:T(8,128)(2,1)S(1)}, bf16[128,768]{1,0:T(8,128)(2,1)}, u32[]{:S(2)}) copy-start(bf16[128,768]{1,0:T(8,128)(2,1)} %constant.40.clone.back) | copy-start | bytes 589828
  36.2 1.2 %copy-start.3 = (f32[4096]{0:T(1024)S(1)}, f32[4096]{0:T(1024)}, u32[]{:S(2)}) copy-start(f32[4096]{0:T(1024)} %param.9) | copy-start | bytes 49156
  42.7 4.7 %collective-permute-start.12 = (bf16[128,768]{1,0:T(8,128)(2,1)S(1)}, bf16[128,768]{1,0:T(8,128)(2,1)S(1)}, u32[]{:S(2)}, u32[]{:S(2)}) collective-permute-start(bf16[128,768]{1,0:T(8,128)(2,1)S(1)} %get-tuple-element.105), channel_id=1, source_target_pairs={{0,2},{2,0},{4,6},{6,4},{8,10},{10,8},{12,14},{14,12},{16,18},{18,... | collective-permute-start | bytes 589832 | tf_op jit(solution)/shard_map/ppermute | solution.py:309
  45.8 1.6 %collective-permute-start.11 = (bf16[128,768]{1,0:T(8,128)(2,1)S(1)}, bf16[128,768]{1,0:T(8,128)(2,1)S(1)}, u32[]{:S(2)}, u32[]{:S(2)}) collective-permute-start(bf16[128,768]{1,0:T(8,128)(2,1)S(1)} %get-tuple-element.104), channel_id=1, source_target_pairs={{0,2},{2,0},{4,6},{6,4},{8,10},{10,8},{12,14},{14,12},{16,18},{18,... | collective-permute-start | bytes 589832 | tf_op jit(solution)/shard_map/ppermute | solution.py:309
  45.8 1.6 %collective-permute-start.13 = (bf16[128,512]{1,0:T(8,128)(2,1)S(1)}, bf16[128,512]{1,0:T(8,128)(2,1)S(1)}, u32[]{:S(2)}, u32[]{:S(2)}) collective-permute-start(bf16[128,512]{1,0:T(8,128)(2,1)S(1)} %get-tuple-element.106), channel_id=1, source_target_pairs={{0,2},{2,0},{4,6},{6,4},{8,10},{10,8},{12,14},{14,12},{16,18},{18,... | collective-permute-start | bytes 393224 | tf_op jit(solution)/shard_map/ppermute | solution.py:309

commit v4 on v3

--- a/solution.py
+++ b/solution.py
@@ -12,7 +12,8 @@
 BF16 = jnp.bfloat16
 F32 = jnp.float32
 EPS = 1e-06
-CFG = dict(tile=256, cuts=(6, 6), g=1, hk=1, t=0, w=0, p=0, s=1, f=1, l=0)
+CUTS = (5, 6)
+TILE = 768
 GROUP = 4
 LANES = 128
 PARTS = 3
@@ -205,9 +206,10 @@
         store(sum1_out, part, sums[1])
 
 
-def second_body(total_channels, tile, start, raw, core, forward, back, own, far, near, *rest):
+def second_body(total_channels, tile, start, raw, fused, core, forward, back, own, far, near, *rest):
     packed = rest[:3] if raw else (None, None, None)
-    last, skip, gate, given_gate, sum0, sum1, *h, own_out, given_out = rest[3:] if raw else rest
+    last, skip, gate, given_gate, *rest, own_out, given_out = rest[3:] if raw else rest
+    kept, h = ([], rest) if fused else (rest[:2], rest[2:])
     half = gate.shape[1] // 2
     table = forward[...]
     rows = table.shape[0] // 2
@@ -225,8 +227,17 @@
         local = slice(start + k * tile, start + (k + 1) * tile)
         wide = pl.ds(pl.multiple_of(first + k * tile, LANES), tile)
         near0, near1 = (spectrum(table, b) for b in blocks(total_channels, rows, near, part, packed[2]))
-        sums = near_terms(near0, near1, (load(sum0, part), load(sum1, part)), h, local)
-        here, there = blocks(total_channels, rows, own, part, packed[0]), blocks(total_channels, rows, far, part, packed[1])
+        here, there = (
+            blocks(total_channels, rows, block, part, by) for block, by in zip((own, far), packed)
+        )
+        if fused:
+            own0, own1, far0, far1 = (spectrum(table, block) for block in (*here, *there))
+            same, next_ = load(h[0], local), load(h[1], local)
+            sums = times(own0, same), plus(times(own1, same), times(own0, next_))
+            sums = far_terms(far0, far1, sums, h, local)
+        else:
+            sums = [load(sum_, part) for sum_ in kept]
+        sums = near_terms(near0, near1, sums, h, local)
         values = []
         for j in range(2):
             value = restored(sums[j]) + last[:, wide] * there[j].astype(F32)
@@ -255,7 +266,7 @@
 
 def tile_of(width):
     best = LANES
-    for tile in range(LANES, CFG["tile"] + 1, LANES):
+    for tile in range(LANES, TILE + 1, LANES):
         if width % tile == 0:
             best = tile
     return best
@@ -292,7 +303,7 @@
     shape = jax.ShapeDtypeStruct((forward.shape[0] // 2, width), BF16)
     operands = [core, forward, back, *blocks, *packed, *small, *gates, *sums, *h]
     return pl.pallas_call(
-        functools.partial(second_body, total_channels, tile_of(width), start, bool(packed)),
+        functools.partial(second_body, total_channels, tile_of(width), start, bool(packed), not sums),
         in_specs=[SMEM] + [VMEM] * (len(operands) - 1),
         out_specs=[VMEM] * 2,
         out_shape=[shape] * 2,
@@ -331,7 +342,7 @@
     tie = lax.optimization_barrier
 
     units = half // LANES
-    cuts = [max(1, units * c // 16) for c in CFG["cuts"]]
+    cuts = [max(1, units * c // 16) for c in CUTS]
     cuts.append(units - sum(cuts))
     cuts = [c * LANES for c in cuts]
     starts = [sum(cuts[:k]) for k in range(len(cuts))]
@@ -359,15 +370,9 @@
 
     own = [None, None, gathered(2, mine)]
     straight = shifted(own[2], 2)
-    if CFG["t"] == 2:
-        squares, own[2] = tie((squares, own[2]))
     squares = sum_over(squares, "chan")
-    if CFG["t"] >= 1:
-        mine, squares = tie((mine, squares))
     own[0] = gathered(0, mine)
     given_squares = swapped_with(squares, "seq", 1)
-    if CFG["p"]:
-        given_squares, own[0] = tie((given_squares, own[0]))
     own[1] = pl.pallas_call(
         functools.partial(pack_body, total_channels, starts[1]),
         in_specs=[SMEM] + [VMEM] * 4,
@@ -375,8 +380,6 @@
         out_shape=jax.ShapeDtypeStruct((2 * rows + RIDER, cuts[1]), BF16),
         compiler_params=PARAMS,
     )(core_arg, mine, given, squares, given_squares)
-    if CFG["w"]:
-        own[2], own[1] = tie((own[2], own[1]))
     far = [shifted(block, 4) for block in own]
 
     last = long_filter[GROUP * rows :].astype(F32)
@@ -387,35 +390,24 @@
         return swapped_with(jnp.where(on_low, own[k], far[k]), "seq", 2)
 
     far[0], own[1] = tie((far[0], own[1]))
-    if CFG["s"]:
-        far[0], straight = tie((far[0], straight))
-    if CFG["l"]:
-        far[0], last = tie((far[0], last))
+    far[0], straight = tie((far[0], straight))
     near = [turned(0), None, straight]
-    if CFG["hk"] == 1:
-        taps, far[0] = tie((taps, far[0]))
+    taps, far[0] = tie((taps, far[0]))
     h = spectra(core_arg, forward, taps, half)
-    if CFG["hk"] == 1:
-        far[1], h = tie((far[1], h))
+    far[1], h = tie((far[1], h))
     sent = jnp.where(on_low, own[1], far[1])
     near_rider = swapped_with(sent[2 * rows :], "seq", 2)
     near[1] = swapped_with(sent[: 2 * rows], "seq", 2)
-    if CFG["g"] == 1:
-        gating, far[0] = tie((gating, far[0]))
-    if CFG["g"] == 2:
-        gating, far[1] = tie((gating, far[1]))
-    if CFG["g"] == 3:
-        gating, far[2] = tie((gating, far[2]))
+    gating, far[0] = tie((gating, far[0]))
     given_gate = swapped_with(gating, "seq", 1)
-    if CFG["f"] == 0:
-        far[0], far[1], far[2] = tie((far[0], far[1], far[2]))
     sums, made = [None] * 3, [None] * 3
-    for k in range(3):
+    for k in range(2):
         packed = () if k == 1 else (own[1], far[1])
         sums[k] = first_part(total_channels, forward, (own[k], far[k]), packed, h, starts[k], cuts[k])
-        if k < 2:
-            far[k + 1], sums[k] = tie((far[k + 1], sums[k]))
-    near[0], near[2], near_rider, sums[2] = tie((near[0], near[2], near_rider, sums[2]))
+        far[k + 1], sums[k] = tie((far[k + 1], sums[k]))
+    sums[2] = ()
+    near[0], near[2], near_rider, sums[1] = tie((near[0], near[2], near_rider, sums[1]))
+    far[2], near[0] = tie((far[2], near[0]))
     order = (0, 2, 1)
     for j, k in enumerate(order):
         packed = () if k == 1 else (own[1], far[1], near_rider)

time: 48.9 us -> 48.8 us (level)
  waiting for transfers between devices: 8.19 us -> 9.25 us
  Pallas kernels: 15.8 us -> 14.8 us
    pallas_call x3 -> x2, Pallas kernels: 4.14 us -> 2.81 us  [first_part(): pl.pallas_call(functools.partial(first_body, total_channels, tile_of(widt...]
    pallas_call x3, Pallas kernels: 5.24 us -> 6.24 us  [second_part(): pl.pallas_call(functools.partial(second_body, total_channels, tile_of(wid...]
    ppermute x4, waiting for transfers between devices: 3.07 us -> 3.78 us  [shifted(): lax.ppermute(value, 'seq', [(s, s + steps) for s in range(count - steps)])]
    pallas_call x1, Pallas kernels: 3.56 us -> 2.85 us  [spectra(): pl.pallas_call(functools.partial(spectra_body, tile), in_specs=[SMEM, VME...]
  transfers between devices with their start and end apart: 14 -> 14, of which waited for: 7 -> 8; matrix products, arithmetic and copies ran while one was open for 2% -> 2% of each run, Pallas kernels for 24% -> 22%
where the time goes in v4:
time: 48.8 us; the launch traced here: 48.4 us
  starting transfers between devices  23.1 us (47%)
  Pallas kernels  14.8 us (30%)
  waiting for transfers between devices  9.25 us (19%)
  other arithmetic  0.94 us (2%)
    ppermute x10, starting transfers between devices, swapped_with(): lax.ppermute(value, axis, [(s, s ^ bit) for s in range(lax.axis_size(axis...  12.8 us
    ppermute x4, starting transfers between devices, shifted(): lax.ppermute(value, 'seq', [(s, s + steps) for s in range(count - steps)])  10.3 us
    pallas_call x3, Pallas kernels, second_part(): pl.pallas_call(functools.partial(second_body, total_channels, tile_of(wid...  6.24 us
    ppermute x10, waiting for transfers between devices, swapped_with(): lax.ppermute(value, axis, [(s, s ^ bit) for s in range(lax.axis_size(axis...  5.47 us
    ppermute x4, waiting for transfers between devices, shifted(): lax.ppermute(value, 'seq', [(s, s + steps) for s in range(count - steps)])  3.78 us
    pallas_call x1, Pallas kernels, spectra(): pl.pallas_call(functools.partial(spectra_body, tile), in_specs=[SMEM, VME...  2.85 us
    pallas_call x2, Pallas kernels, first_part(): pl.pallas_call(functools.partial(first_body, total_channels, tile_of(widt...  2.81 us
    pallas_call x1, Pallas kernels, on_device(): pl.pallas_call(front_body, in_specs=[SMEM, HBM], out_specs=[VMEM] * 3, ou...  1.54 us
  transfers between devices with their start and end apart: 14, of which 8 were waited for; matrix products, arithmetic and copies ran while one was open for 2% of the time, Pallas kernels for 22%

profile of v4, /device:TPU:17, one launch (start us, length us, event | category | flops | bytes accessed | tf_op | source)
XLA Modules:
  0.0 48.4 jit_solution(1091312591456078387)
XLA Ops:
  0.0 1.5 %shard_map.64 = (f32[8,128]{1,0:T(8,128)S(1)}, bf16[128,2048]{1,0:T(8,128)(2,1)S(1)}, bf16[128,2048]{1,0:T(8,128)(2,1)S(1)}) custom-call(s32[1]{0:T(128)} %bitcast.core, bf16[128,4096]{1,0:T(8,128)(2,1)} %x.1), custom_call_target="tpu_custom_call" | custom-call | tf_op jit(solution)/shard_map/pallas_call | solution.py:351
  1.5 0.7 %collective-permute-start = (bf16[128,2048]{1,0:T(8,128)(2,1)S(1)}, bf16[128,2048]{1,0:T(8,128)(2,1)S(1)}, u32[]{:S(2)}, u32[]{:S(2)}) collective-permute-start(bf16[128,2048]{1,0:T(8,128)(2,1)S(1)} %get-tuple-element.57), channel_id=1, source_target_pairs={{0,2},{2,0},{4,6},{6,4},{8,10},{10,8},{12,14},{14,12},{16,18},{18,... | collective-permute-start | bytes 1572872 | tf_op jit(solution)/shard_map/ppermute | solution.py:320
  2.3 1.5 %collective-permute-done.given = bf16[128,2048]{1,0:T(8,128)(2,1)S(1)} collective-permute-done((bf16[128,2048]{1,0:T(8,128)(2,1)S(1)}, bf16[128,2048]{1,0:T(8,128)(2,1)S(1)}, u32[]{:S(2)}, u32[]{:S(2)}) %collective-permute-start) | collective-permute-done | bytes 524320 | tf_op jit(solution)/shard_map/ppermute | solution.py:320
  3.9 3.3 %collective-permute-start.1 = (bf16[256,640]{1,0:T(8,128)(2,1)S(1)}, bf16[256,640]{1,0:T(8,128)(2,1)S(1)}, u32[]{:S(2)}, u32[]{:S(2)}) collective-permute-start(bf16[256,640]{1,0:T(8,128)(2,1)S(1)} %shard_map.65.own), channel_id=1, source_target_pairs={{0,8},{2,10},{4,12},{6,14},{8,16},{10,18},{12,20},{14,22},{16,24},... | collective-permute-start | bytes 983048 | tf_op jit(solution)/shard_map/ppermute | solution.py:316
  7.3 3.1 %collective-permute-start.4 = (bf16[256,640]{1,0:T(8,128)(2,1)S(1)}, bf16[256,640]{1,0:T(8,128)(2,1)S(1)}, u32[]{:S(2)}, u32[]{:S(2)}) collective-permute-start(bf16[256,640]{1,0:T(8,128)(2,1)S(1)} %shard_map.67.own), channel_id=1, source_target_pairs={{0,4},{2,6},{4,8},{6,10},{8,12},{10,14},{12,16},{14,18},{16,20},{1... | collective-permute-start | bytes 983048 | tf_op jit(solution)/shard_map/ppermute | solution.py:316
  10.4 1.3 %collective-permute-start.2 = (f32[8,128]{1,0:T(8,128)S(1)}, f32[8,128]{1,0:T(8,128)S(1)}, u32[]{:S(2)}, u32[]{:S(2)}) collective-permute-start(f32[8,128]{1,0:T(8,128)S(1)} %get-tuple-element.58), channel_id=1, source_target_pairs={{0,1},{1,0},{2,3},{3,2},{4,5},{5,4},{6,7},{7,6},{8,9},{9,8},{10,11... | collective-permute-start | bytes 12296 | tf_op jit(solution)/shard_map/ppermute | solution.py:320
  11.7 1.5 %collective-permute-done.2 = f32[8,128]{1,0:T(8,128)S(1)} collective-permute-done((f32[8,128]{1,0:T(8,128)S(1)}, f32[8,128]{1,0:T(8,128)S(1)}, u32[]{:S(2)}, u32[]{:S(2)}) %collective-permute-start.2) | collective-permute-done | bytes 4128 | tf_op jit(solution)/shard_map/ppermute | solution.py:320
  13.2 1.8 %collective-permute-start.3 = (f32[8,128]{1,0:T(8,128)S(1)}, f32[8,128]{1,0:T(8,128)S(1)}, u32[]{:S(2)}, u32[]{:S(2)}) collective-permute-start(f32[8,128]{1,0:T(8,128)S(1)} %add.13.squares), channel_id=1, source_target_pairs={{0,2},{2,0},{4,6},{6,4},{8,10},{10,8},{12,14},{14,12},{16,18},{18,... | collective-permute-start | bytes 12296 | tf_op jit(solution)/shard_map/ppermute | solution.py:320
  15.0 0.8 %collective-permute-done.3.given_squares = f32[8,128]{1,0:T(8,128)S(1)} collective-permute-done((f32[8,128]{1,0:T(8,128)S(1)}, f32[8,128]{1,0:T(8,128)S(1)}, u32[]{:S(2)}, u32[]{:S(2)}) %collective-permute-start.3) | collective-permute-done | bytes 4128 | tf_op jit(solution)/shard_map/ppermute | solution.py:320
  15.9 0.2 shard_map.66.rest_0_.own
  16.1 1.9 %collective-permute-start.6 = (bf16[272,768]{1,0:T(8,128)(2,1)S(1)}, bf16[272,768]{1,0:T(8,128)(2,1)S(1)}, u32[]{:S(2)}, u32[]{:S(2)}) collective-permute-start(bf16[272,768]{1,0:T(8,128)(2,1)S(1)} %shard_map.66.rest_0_.own), channel_id=1, source_target_pairs={{0,8},{2,10},{4,12},{6,14},{8,16},{10,18},{12,20},{14,22},{16,24},... | collective-permute-start | bytes 1253384 | tf_op jit(solution)/shard_map/ppermute | solution.py:316
  18.1 1.9 %collective-permute-start.8 = (bf16[256,640]{1,0:T(8,128)(2,1)S(1)}, bf16[256,640]{1,0:T(8,128)(2,1)S(1)}, u32[]{:S(2)}, u32[]{:S(2)}) collective-permute-start(bf16[256,640]{1,0:T(8,128)(2,1)S(1)} %shard_map.67.own), channel_id=1, source_target_pairs={{0,8},{2,10},{4,12},{6,14},{8,16},{10,18},{12,20},{14,22},{16,24},... | collective-permute-start | bytes 983048 | tf_op jit(solution)/shard_map/ppermute | solution.py:316
  20.0 2.8 %collective-permute-done.4.near = bf16[256,640]{1,0:T(8,128)(2,1)S(1)} collective-permute-done((bf16[256,640]{1,0:T(8,128)(2,1)S(1)}, bf16[256,640]{1,0:T(8,128)(2,1)S(1)}, u32[]{:S(2)}, u32[]{:S(2)}) %collective-permute-start.4) | collective-permute-done | bytes 327712 | tf_op jit(solution)/shard_map/ppermute | solution.py:316
  22.8 0.1 collective-permute-start.5
  22.9 2.1 %collective-permute-start.9 = (bf16[128,4096]{1,0:T(8,128)(2,1)S(1)}, bf16[128,4096]{1,0:T(8,128)(2,1)S(1)}, u32[]{:S(2)}, u32[]{:S(2)}) collective-permute-start(bf16[128,4096]{1,0:T(8,128)(2,1)S(1)} %copy-done), channel_id=1, source_target_pairs={{0,2},{2,0},{4,6},{6,4},{8,10},{10,8},{12,14},{14,12},{16,18},{18,... | collective-permute-start | bytes 3145736 | tf_op jit(solution)/shard_map/ppermute | solution.py:320
  25.0 2.9 %shard_map.68 = (f32[256,2048]{1,0:T(8,128)S(1)}, f32[256,2048]{1,0:T(8,128)S(1)}, f32[256,2048]{1,0:T(8,128)S(1)}, f32[256,2048]{1,0:T(8,128)S(1)}, f32[256,2048]{1,0:T(8,128)S(1)}) custom-call(s32[1]{0:T(128)} %bitcast.core, bf16[256,256]{1,0:T(8,128)(2,1)S(1)} %copy-done.1, bf16[513,4096]{1,0:T(8,128)(2,1)} %taps), custom_call_target="tpu_custom_call" | custom-call | tf_op jit(solution)/shard_map/pallas_call | solution.py:278
  27.9 1.0 %collective-permute-done.6.rest_1_.far = bf16[272,768]{1,0:T(8,128)(2,1)S(1)} collective-permute-done((bf16[272,768]{1,0:T(8,128)(2,1)S(1)}, bf16[272,768]{1,0:T(8,128)(2,1)S(1)}, u32[]{:S(2)}, u32[]{:S(2)}) %collective-permute-start.6) | collective-permute-done | bytes 417824 | tf_op jit(solution)/shard_map/ppermute | solution.py:316
  29.0 3.2 %collective-permute-start.7 = (bf16[16,768]{1,0:T(8,128)(2,1)S(1)}, bf16[16,768]{1,0:T(8,128)(2,1)S(1)}, u32[]{:S(2)}, u32[]{:S(2)}) collective-permute-start(bf16[16,768]{1,0:T(8,128)(2,1)S(1)} %slice.12), channel_id=1, source_target_pairs={{0,4},{2,6},{4,0},{6,2},{8,12},{10,14},{12,8},{14,10},{16,20},{18,... | collective-permute-start | bytes 73736 | tf_op jit(solution)/shard_map/ppermute | solution.py:320
  32.2 0.1 collective-permute-start.10
  32.3 0.8 %slice_convert_fusion.rest_3_.rest_0_ = f32[1,4096]{1,0:T(1,128)S(1)} fusion(bf16[513,4096]{1,0:T(8,128)(2,1)} %taps), kind=kLoop, calls=%fused_computation.2 | loop fusion | flops 4096 | bytes 24576 | tf_op jit(solution)/shard_map/convert_element_type | solution.py:385
  33.1 1.4 %shard_map.69 = (f32[256,640]{1,0:T(8,128)S(1)}, f32[256,640]{1,0:T(8,128)S(1)}) custom-call(bf16[256,256]{1,0:T(8,128)(2,1)S(1)} %copy-done.1, bf16[256,640]{1,0:T(8,128)(2,1)S(1)} %shard_map.65.own, bf16[256,640]{1,0:T(8,128)(2,1)S(1)} %collective-permute-done.1.far, bf16[272,768]{1,0:T(8,128)(2,1)S(1)} %shard_map.66.rest_0_.own, ...), custom_call_target="tpu_custom_call" | custom-call | tf_op jit(solution)/shard_map/pallas_call | solution.py:293
  34.5 1.4 %shard_map.70 = (f32[256,768]{1,0:T(8,128)S(1)}, f32[256,768]{1,0:T(8,128)S(1)}) custom-call(bf16[256,256]{1,0:T(8,128)(2,1)S(1)} %copy-done.1, bf16[272,768]{1,0:T(8,128)(2,1)S(1)} %shard_map.66.rest_0_.own, bf16[272,768]{1,0:T(8,128)(2,1)S(1)} %collective-permute-done.6.rest_1_.far, ...), custom_call_target="tpu_custom_call" | custom-call | tf_op jit(solution)/shard_map/pallas_call | solution.py:293
  36.0 1.7 %shard_map.71 = (bf16[128,640]{1,0:T(8,128)(2,1)S(1)}, bf16[128,640]{1,0:T(8,128)(2,1)S(1)}) custom-call(s32[1]{0:T(128)} %bitcast.core, bf16[256,256]{1,0:T(8,128)(2,1)S(1)} %copy-done.1, bf16[128,768]{1,0:T(8,128)(2,1)S(1)} %copy-done.2, bf16[256,640]{1,0:T(8,128)(2,1)S(1)} %shard_map.65.own, bf16[256,640]{1,0:T(8,128)(2,1)S(1)} %collective-permute-done.1.far, ...), custom_call_target="tpu_custom_call" | custom-call | tf_op jit(solution)/shard_map/pallas_call | solution.py:305
  37.8 2.8 %shard_map.72 = (bf16[128,640]{1,0:T(8,128)(2,1)S(1)}, bf16[128,640]{1,0:T(8,128)(2,1)S(1)}) custom-call(s32[1]{0:T(128)} %bitcast.core, bf16[256,256]{1,0:T(8,128)(2,1)S(1)} %copy-done.1, bf16[128,768]{1,0:T(8,128)(2,1)S(1)} %copy-done.2, bf16[256,640]{1,0:T(8,128)(2,1)S(1)} %shard_map.67.own, bf16[256,640]{1,0:T(8,128)(2,1)S(1)} %collective-permute-done.8.far, ...), custom_call_target="tpu_custom_call" | custom-call | tf_op jit(solution)/shard_map/pallas_call | solution.py:305
  40.6 0.4 collective-permute-done.10.near
  41.0 1.7 %shard_map.73 = (bf16[128,768]{1,0:T(8,128)(2,1)S(1)}, bf16[128,768]{1,0:T(8,128)(2,1)S(1)}) custom-call(s32[1]{0:T(128)} %bitcast.core, bf16[256,256]{1,0:T(8,128)(2,1)S(1)} %copy-done.1, bf16[128,768]{1,0:T(8,128)(2,1)S(1)} %copy-done.2, bf16[272,768]{1,0:T(8,128)(2,1)S(1)} %shard_map.66.rest_0_.own, ...), custom_call_target="tpu_custom_call" | custom-call | tf_op jit(solution)/shard_map/pallas_call | solution.py:305
  42.7 3.0 %collective-permute-start.12 = (bf16[128,768]{1,0:T(8,128)(2,1)S(1)}, bf16[128,768]{1,0:T(8,128)(2,1)S(1)}, u32[]{:S(2)}, u32[]{:S(2)}) collective-permute-start(bf16[128,768]{1,0:T(8,128)(2,1)S(1)} %get-tuple-element.105), channel_id=1, source_target_pairs={{0,2},{2,0},{4,6},{6,4},{8,10},{10,8},{12,14},{14,12},{16,18},{18,... | collective-permute-start | bytes 589832 | tf_op jit(solution)/shard_map/ppermute | solution.py:320
  45.8 0.1 collective-permute-start.13
  45.9 0.4 collective-permute-start.11
  46.3 0.9 %collective-permute-done.13.rest_5_ = bf16[128,640]{1,0:T(8,128)(2,1)S(1)} collective-permute-done((bf16[128,640]{1,0:T(8,128)(2,1)S(1)}, bf16[128,640]{1,0:T(8,128)(2,1)S(1)}, u32[]{:S(2)}, u32[]{:S(2)}) %collective-permute-start.13) | collective-permute-done | bytes 163872 | tf_op jit(solution)/shard_map/ppermute | solution.py:320
  47.2 0.2 collective-permute-done.11.rest_3_
  47.4 1.0 %shard_map.74 = bf16[128,4096]{1,0:T(8,128)(2,1)} custom-call(s32[1]{0:T(128)} %bitcast.core, bf16[128,640]{1,0:T(8,128)(2,1)S(1)} %get-tuple-element.94.rest_0_, bf16[128,768]{1,0:T(8,128)(2,1)S(1)} %get-tuple-element.102.rest_1_, bf16[128,640]{1,0:T(8,128)(2,1)S(1)} %get-tuple-element.103.rest_2_, bf16[128,640]{1,0:T(8,128)(2,1)S(1)} %collective-permute-done.11.rest_3_, ...), custom_call_target="tpu_custom_call" | custom-call | tf_op jit(solution)/shard_map/pallas_call | solution.py:422
  (21 shorter events, 0.2 us)
Async XLA Ops:
  1.5 2.3 %collective-permute-start = (bf16[128,2048]{1,0:T(8,128)(2,1)S(1)}, bf16[128,2048]{1,0:T(8,128)(2,1)S(1)}, u32[]{:S(2)}, u32[]{:S(2)}) collective-permute-start(bf16[128,2048]{1,0:T(8,128)(2,1)S(1)} %get-tuple-element.57), channel_id=1, source_target_pairs={{0,2},{2,0},{4,6},{6,4},{8,10},{10,8},{12,14},{14,12},{16,18},{18,... | collective-permute-start | bytes 1572872 | tf_op jit(solution)/shard_map/ppermute | solution.py:320
  3.9 19.1 %copy-start = (bf16[128,4096]{1,0:T(8,128)(2,1)S(1)}, bf16[128,4096]{1,0:T(8,128)(2,1)}, u32[]{:S(2)}) copy-start(bf16[128,4096]{1,0:T(8,128)(2,1)} %rest_2_) | copy-start | bytes 3145732
  3.9 21.2 %copy-start.1 = (bf16[256,256]{1,0:T(8,128)(2,1)S(1)}, bf16[256,256]{1,0:T(8,128)(2,1)}, u32[]{:S(2)}) copy-start(bf16[256,256]{1,0:T(8,128)(2,1)} %constant.39.clone.forward) | copy-start | bytes 393220
  3.9 16.1 %collective-permute-start.1 = (bf16[256,640]{1,0:T(8,128)(2,1)S(1)}, bf16[256,640]{1,0:T(8,128)(2,1)S(1)}, u32[]{:S(2)}, u32[]{:S(2)}) collective-permute-start(bf16[256,640]{1,0:T(8,128)(2,1)S(1)} %shard_map.65.own), channel_id=1, source_target_pairs={{0,8},{2,10},{4,12},{6,14},{8,16},{10,18},{12,20},{14,22},{16,24},... | collective-permute-start | bytes 983048 | tf_op jit(solution)/shard_map/ppermute | solution.py:316
  7.3 15.5 %collective-permute-start.4 = (bf16[256,640]{1,0:T(8,128)(2,1)S(1)}, bf16[256,640]{1,0:T(8,128)(2,1)S(1)}, u32[]{:S(2)}, u32[]{:S(2)}) collective-permute-start(bf16[256,640]{1,0:T(8,128)(2,1)S(1)} %shard_map.67.own), channel_id=1, source_target_pairs={{0,4},{2,6},{4,8},{6,10},{8,12},{10,14},{12,16},{14,18},{16,20},{1... | collective-permute-start | bytes 983048 | tf_op jit(solution)/shard_map/ppermute | solution.py:316
  10.4 2.8 %collective-permute-start.2 = (f32[8,128]{1,0:T(8,128)S(1)}, f32[8,128]{1,0:T(8,128)S(1)}, u32[]{:S(2)}, u32[]{:S(2)}) collective-permute-start(f32[8,128]{1,0:T(8,128)S(1)} %get-tuple-element.58), channel_id=1, source_target_pairs={{0,1},{1,0},{2,3},{3,2},{4,5},{5,4},{6,7},{7,6},{8,9},{9,8},{10,11... | collective-permute-start | bytes 12296 | tf_op jit(solution)/shard_map/ppermute | solution.py:320
  13.2 2.6 %collective-permute-start.3 = (f32[8,128]{1,0:T(8,128)S(1)}, f32[8,128]{1,0:T(8,128)S(1)}, u32[]{:S(2)}, u32[]{:S(2)}) collective-permute-start(f32[8,128]{1,0:T(8,128)S(1)} %add.13.squares), channel_id=1, source_target_pairs={{0,2},{2,0},{4,6},{6,4},{8,10},{10,8},{12,14},{14,12},{16,18},{18,... | collective-permute-start | bytes 12296 | tf_op jit(solution)/shard_map/ppermute | solution.py:320
  16.1 12.8 %collective-permute-start.6 = (bf16[272,768]{1,0:T(8,128)(2,1)S(1)}, bf16[272,768]{1,0:T(8,128)(2,1)S(1)}, u32[]{:S(2)}, u32[]{:S(2)}) collective-permute-start(bf16[272,768]{1,0:T(8,128)(2,1)S(1)} %shard_map.66.rest_0_.own), channel_id=1, source_target_pairs={{0,8},{2,10},{4,12},{6,14},{8,16},{10,18},{12,20},{14,22},{16,24},... | collective-permute-start | bytes 1253384 | tf_op jit(solution)/shard_map/ppermute | solution.py:316
  18.1 17.9 %collective-permute-start.8 = (bf16[256,640]{1,0:T(8,128)(2,1)S(1)}, bf16[256,640]{1,0:T(8,128)(2,1)S(1)}, u32[]{:S(2)}, u32[]{:S(2)}) collective-permute-start(bf16[256,640]{1,0:T(8,128)(2,1)S(1)} %shard_map.67.own), channel_id=1, source_target_pairs={{0,8},{2,10},{4,12},{6,14},{8,16},{10,18},{12,20},{14,22},{16,24},... | collective-permute-start | bytes 983048 | tf_op jit(solution)/shard_map/ppermute | solution.py:316
  22.8 13.2 %collective-permute-start.5 = (bf16[256,640]{1,0:T(8,128)(2,1)S(1)}, bf16[256,640]{1,0:T(8,128)(2,1)S(1)}, u32[]{:S(2)}, u32[]{:S(2)}) collective-permute-start(bf16[256,640]{1,0:T(8,128)(2,1)S(1)} %broadcast_select_fusion.1), channel_id=1, source_target_pairs={{0,4},{2,6},{4,0},{6,2},{8,12},{10,14},{12,8},{14,10},{16,20},{18,... | collective-permute-start | bytes 983048 | tf_op jit(solution)/shard_map/ppermute | solution.py:320
  22.9 13.1 %collective-permute-start.9 = (bf16[128,4096]{1,0:T(8,128)(2,1)S(1)}, bf16[128,4096]{1,0:T(8,128)(2,1)S(1)}, u32[]{:S(2)}, u32[]{:S(2)}) collective-permute-start(bf16[128,4096]{1,0:T(8,128)(2,1)S(1)} %copy-done), channel_id=1, source_target_pairs={{0,2},{2,0},{4,6},{6,4},{8,10},{10,8},{12,14},{14,12},{16,18},{18,... | collective-permute-start | bytes 3145736 | tf_op jit(solution)/shard_map/ppermute | solution.py:320
  29.0 7.0 %collective-permute-start.7 = (bf16[16,768]{1,0:T(8,128)(2,1)S(1)}, bf16[16,768]{1,0:T(8,128)(2,1)S(1)}, u32[]{:S(2)}, u32[]{:S(2)}) collective-permute-start(bf16[16,768]{1,0:T(8,128)(2,1)S(1)} %slice.12), channel_id=1, source_target_pairs={{0,4},{2,6},{4,0},{6,2},{8,12},{10,14},{12,8},{14,10},{16,20},{18,... | collective-permute-start | bytes 73736 | tf_op jit(solution)/shard_map/ppermute | solution.py:320
  32.2 8.8 %collective-permute-start.10 = (bf16[256,768]{1,0:T(8,128)(2,1)S(1)}, bf16[256,768]{1,0:T(8,128)(2,1)S(1)}, u32[]{:S(2)}, u32[]{:S(2)}) collective-permute-start(bf16[256,768]{1,0:T(8,128)(2,1)S(1)} %slice.13), channel_id=1, source_target_pairs={{0,4},{2,6},{4,0},{6,2},{8,12},{10,14},{12,8},{14,10},{16,20},{18,... | collective-permute-start | bytes 1179656 | tf_op jit(solution)/shard_map/ppermute | solution.py:320
  34.5 1.5 %copy-start.2 = (bf16[128,768]{1,0:T(8,128)(2,1)S(1)}, bf16[128,768]{1,0:T(8,128)(2,1)}, u32[]{:S(2)}) copy-start(bf16[128,768]{1,0:T(8,128)(2,1)} %constant.40.clone.back) | copy-start | bytes 589828
  34.5 1.5 %copy-start.3 = (f32[4096]{0:T(1024)S(1)}, f32[4096]{0:T(1024)}, u32[]{:S(2)}) copy-start(f32[4096]{0:T(1024)} %param.9) | copy-start | bytes 49156
  42.7 4.7 %collective-permute-start.12 = (bf16[128,768]{1,0:T(8,128)(2,1)S(1)}, bf16[128,768]{1,0:T(8,128)(2,1)S(1)}, u32[]{:S(2)}, u32[]{:S(2)}) collective-permute-start(bf16[128,768]{1,0:T(8,128)(2,1)S(1)} %get-tuple-element.105), channel_id=1, source_target_pairs={{0,2},{2,0},{4,6},{6,4},{8,10},{10,8},{12,14},{14,12},{16,18},{18,... | collective-permute-start | bytes 589832 | tf_op jit(solution)/shard_map/ppermute | solution.py:320
  45.8 1.4 %collective-permute-start.13 = (bf16[128,640]{1,0:T(8,128)(2,1)S(1)}, bf16[128,640]{1,0:T(8,128)(2,1)S(1)}, u32[]{:S(2)}, u32[]{:S(2)}) collective-permute-start(bf16[128,640]{1,0:T(8,128)(2,1)S(1)} %get-tuple-element.106), channel_id=1, source_target_pairs={{0,2},{2,0},{4,6},{6,4},{8,10},{10,8},{12,14},{14,12},{16,18},{18,... | collective-permute-start | bytes 491528 | tf_op jit(solution)/shard_map/ppermute | solution.py:320
  45.9 1.6 %collective-permute-start.11 = (bf16[128,640]{1,0:T(8,128)(2,1)S(1)}, bf16[128,640]{1,0:T(8,128)(2,1)S(1)}, u32[]{:S(2)}, u32[]{:S(2)}) collective-permute-start(bf16[128,640]{1,0:T(8,128)(2,1)S(1)} %get-tuple-element.104), channel_id=1, source_target_pairs={{0,2},{2,0},{4,6},{6,4},{8,10},{10,8},{12,14},{14,12},{16,18},{18,... | collective-permute-start | bytes 491528 | tf_op jit(solution)/shard_map/ppermute | solution.py:320
